TPU v7x, 512 devices: a whole 4x4x16 slice. The times are simulated.
512 devices in a mesh: sect: 2 (over z_hi), tp: 32 (over x, z_lo), grp: 8 (over y, core).
Axes of the slice: x: 4, y: 4, z: 16 (z_hi: 2, z_lo: 8; z = z_hi * 8 + z_lo), core: 2. Of those that a mesh axis runs over, the one named last changes fastest.
Arguments:
- mamba_x: bfloat16 [4096, 16384], P(('sect', 'grp'), 'tp'), may hold values from -6 to 6
- mamba_z: bfloat16 [4096, 16384], P(('sect', 'grp'), 'tp'), may hold values from -6 to 6
- conv_weight: float32 [4, 16384], P(None, 'tp'), may hold values from -3 to 3
- conv_bias: float32 [16384], P('tp'), may hold values from -3 to 3
- x_proj: bfloat16 [16384, 544], P('tp'), may hold values from -0.046875 to 0.046875
- norm_gain: float32 [544], replicated, may hold values from 0.5 to 1.5
- dt_proj: bfloat16 [512, 16384], P(None, 'tp'), may hold values from -0.25 to 0.25
- dt_bias: float32 [16384], P('tp'), may hold values from -4 to 0
- a_log: float32 [16, 16384], P(None, 'tp'), may hold values from -3 to 1
- d_skip: float32 [16384], P('tp'), may hold values from 0.5 to 1.5
- segment_ids: int32 [2, 2048], P('sect', 'grp'), may hold values from 0 to 3, never falling along the last dimension, each value on 1 to 1536 neighbouring positions
- queries: bfloat16 [4096, 8192], P(('sect', 'grp'), 'tp'), may hold values from -6 to 6
- keys_values: bfloat16 [4096, 2, 1024], P(('sect', 'grp')), may hold values from -6 to 6
- kv_owner: int32 [2, 128, 1], P('sect', 'grp'), may hold values from 0 to 7; in each aligned block of 16 rows (0 to 15, 16 to 31, ..., all dimensions but the last counted through in order) at most 4 rows name the same one
- moe_in: bfloat16 [4096, 8192], P(('sect', 'grp'), 'tp'), may hold values from -6 to 6
- moe_gain: float32 [8192], P('tp'), may hold values from 0.5 to 1.5
- router: bfloat16 [8192, 16], P('tp'), may hold values from -0.0625 to 0.0625
- routing: int32 [4096, 2], P(('sect', 'grp')), may hold values from 0 to 15, all different within a row
Outputs:
- mixer_out: bfloat16 [4096, 16384], P(('sect', 'grp'), 'tp')
- final_state: float32 [2, 16, 16384], P('sect', 'grp', 'tp')
- attn_out: bfloat16 [4096, 8192], P(('sect', 'grp'), 'tp')
- kv_pages: bfloat16 [2, 8, 32, 32, 16, 256], P('sect', 'grp', 'tp')
- expert_input: bfloat16 [4096, 8192], P(('sect', 'grp'), 'tp')
- gate_weights: float32 [4096, 2], P(('sect', 'grp'))
Inputs may be any that keep to these rules, and one draw needn't show every extreme that they name: `segment_ids`: in each span, ids never fall, start at 0 and number its 4 requests; a request holds at most 1536 positions and one holds exactly that many. `kv_owner`: owner index along grp in the other section. Of the 16 pages of one device's rows, at most 4 share an owner, and in every draw some device has 4 pages for one owner. `routing`: the 2 experts of a token differ.
All inputs are finite; a program needn't handle non-finite values.
Results may differ from a plain program's by a relative error of at most 0.013.
Values may be sent and summed in bfloat16 or wider, within the bound.
A program may use at most 64 MiB of HBM per device.

v0:
```python
import jax
import jax.numpy as jnp
from jax import lax
from jax.experimental import pallas as pl
from jax.experimental.pallas import tpu as pltpu
from jax.sharding import PartitionSpec as P

MESH = pl.DeviceIdType.MESH
F32 = jnp.float32
BF16 = jnp.bfloat16
I32 = jnp.int32

ROWS = 256
WIDTH = 512
RANK = 512
NST = 16
HD = 128
BLK = 16
LANES = 128
NX, NZ, NG = 4, 8, 8
PAY = 768
HALF = PAY // 2
SLOTS = 4
FEATURES = 8192
EPS = 1e-06
LOG2E = 1.4426950408889634
HUGE = 1e30
VMEM = pl.BlockSpec(memory_space=pltpu.VMEM)
ANY = pl.BlockSpec(memory_space=pl.ANY)
DMA = pltpu.SemaphoreType.DMA


def iota(shape, dim):
    return lax.broadcasted_iota(I32, shape, dim)


def dot(a, b, **kw):
    return jnp.dot(a, b, preferred_element_type=F32, **kw)


def dot_t(a, b, **kw):
    return lax.dot_general(a, b, (((1,), (1,)), ((), ())), preferred_element_type=F32, **kw)


def remote(src, dst, send, recv, where):
    return pltpu.make_async_remote_copy(
        src_ref=src, dst_ref=dst, send_sem=send, recv_sem=recv, device_id=where, device_id_type=MESH
    )


INPUTS = (
    ("x", (ROWS, WIDTH), BF16),
    ("seg", (1, ROWS), I32),
    ("conv_w", (4, WIDTH), F32),
    ("conv_b", (1, WIDTH), F32),
    ("proj", (RANK + 2 * NST, WIDTH), BF16),
    ("owner", (1, 16), I32),
    ("page", (ROWS, 2, HD), BF16),
    ("pair", (ROWS, 2, HD), BF16),
    ("moe", (ROWS, 256), BF16),
    ("moe_gain", (1, 256), F32),
    ("router", (16, 256), BF16),
    ("q", (ROWS, 2 * HD), BF16),
    ("z", (ROWS, WIDTH), BF16),
    ("gain", (1, RANK + 2 * NST), F32),
    ("dt", (RANK, WIDTH), BF16),
    ("dt_bias", (1, WIDTH), F32),
    ("a_log", (NST, WIDTH), F32),
    ("skip", (1, WIDTH), F32),
    ("routing", (2, ROWS), I32),
)
OUTPUTS = (
    ("mixed", (ROWS, WIDTH), BF16),
    ("final", (2, WIDTH), F32),
    ("attn", (ROWS, 2 * HD), BF16),
    ("pages", (NG, SLOTS, BLK, 2 * HD), BF16),
    ("expert", (ROWS, 256), BF16),
    ("gate", (2, ROWS), F32),
)
OPERANDS = [n for n, _, _ in INPUTS if n not in ("page", "pair")] + ["keys_values"]
SCRATCH = (
    ("page", (ROWS, 2 * HD), BF16),
    ("pair", (ROWS, 2 * HD), BF16),
    ("rim", (16, WIDTH), BF16),
    ("rim_seg", (8, LANES), F32),
    ("seg_send", (8, LANES), F32),
    ("seg_out", (8, ROWS), F32),
    ("seg_all", (NG, 8, ROWS), F32),
    ("kv_all", (NG, ROWS, 2 * HD), BF16),
    ("ext", (8 + ROWS, WIDTH), F32),
    ("ext_seg", (8 + ROWS, LANES), F32),
    ("conv", (ROWS, WIDTH), BF16),
    ("pay", (ROWS, PAY), BF16),
    ("rx", (2, NX, 64, HALF), BF16),
    ("chunk", (NZ, 16, HALF), BF16),
    ("rz", (NZ, 16, HALF), BF16),
    ("low", (NX, NZ, 16, HALF), BF16),
    ("outgoing", (NG, BLK, 2 * HD), BF16),
    ("best", (2, ROWS, LANES), F32),
    ("accum", (2, ROWS, 2 * HD), F32),
    ("silu_z", (ROWS, WIDTH), F32),
    ("rank", (ROWS, RANK), BF16),
    ("bc", (ROWS, 2 * NST), BF16),
    ("step", (ROWS, WIDTH), F32),
    ("driven", (ROWS, WIDTH), BF16),
    ("b_tiled", (256, ROWS), F32),
    ("c_blocks", (ROWS, 256), BF16),
    ("forced", (256, WIDTH), F32),
    ("states", (256, WIDTH), BF16),
    ("growth", (16, 256, WIDTH), BF16),
    ("rows_out", (ROWS, WIDTH), F32),
    ("ends", (NG, 80, LANES), BF16),
    ("own_end", (80, LANES), BF16),
    ("own_final", (NG, 8, LANES), F32),
    ("landed", (8, LANES), F32),
)
SEMS = (
    ("load", (len(INPUTS),)), ("store", (len(OUTPUTS),)),
    ("rim_s", ()), ("rim_r", ()), ("rseg_s", ()), ("rseg_r", ()),
    ("kv_s", (NG,)), ("kv_r", (NG,)), ("sg_s", (NG,)), ("sg_r", (NG,)),
    ("pg_s", (NG,)), ("pg_r", (NG,)), ("pf_s", (4,)), ("pf_r", (4,)),
    ("x_s", (2, NX)), ("x_r", (2, NX)), ("z_s", (NZ,)), ("z_r", (NZ,)),
    ("g_s", (NZ,)), ("g_r", (NZ,)), ("h_s", (NZ, NX)), ("h_r", (NX, NZ)),
    ("e_s", (NG,)), ("e_r", (NG,)), ("f_s", ()), ("f_r", ()),
)


class Refs:
    pass


def main_kernel(*refs):
    k = Refs()
    names = ["hbm_" + n for n in OPERANDS] + ["hbm_out_" + n for n, _, _ in OUTPUTS]
    names += [n for n, _, _ in SCRATCH] + ["in_" + n for n, _, _ in INPUTS]
    names += ["out_" + n for n, _, _ in OUTPUTS if n != "pages"] + [n for n, _ in SEMS]
    for name, ref in zip(names, refs, strict=True):
        setattr(k, name, ref)
    k.out_pages = k.hbm_out_pages
    sect, tp, grp = lax.axis_index("sect"), lax.axis_index("tp"), lax.axis_index("grp")
    x, z = tp // NZ, tp % NZ
    heads = {"pair": tp // 4, "page": 2 * x + (NZ - 1 - z) // 4}
    loads = {}
    for i, (n, _, _) in enumerate(INPUTS):
        if n in heads:
            src = k.hbm_keys_values.at[:, :, pl.ds(pl.multiple_of(heads[n] * HD, HD), HD)]
        else:
            src = getattr(k, "hbm_" + n)
        loads[n] = pltpu.make_async_copy(src, getattr(k, "in_" + n), k.load.at[i])
        loads[n].start()
    stores = {}
    for i, (n, _, _) in enumerate(OUTPUTS):
        if n != "pages":
            stores[n] = pltpu.make_async_copy(getattr(k, "out_" + n), getattr(k, "hbm_out_" + n), k.store.at[i])

    quad = z // 4 * 4
    others_x = [lax.rem(x + d, NX) for d in range(1, NX)]
    others_z = [lax.rem(z + d, NZ) for d in range(1, NZ)]
    others_q = [quad + lax.rem(z + d, 4) for d in range(1, 4)]
    others_g = [lax.rem(grp + d, NG) for d in range(1, NG)]
    place_x = [{"tp": o * NZ + z} for o in others_x]
    place_z = [{"tp": x * NZ + o} for o in others_z]
    place_q = [{"tp": x * NZ + o} for o in others_q]
    place_g = [{"grp": o} for o in others_g]
    place_p = [{"sect": 1 - sect, "tp": x * NZ + (NZ - 1 - z), "grp": o} for o in range(NG)]
    across = {"sect": 1 - sect}
    partners = place_x + place_z + place_g + place_p + [across]
    barrier = pltpu.get_barrier_semaphore()
    for place in partners:
        pl.semaphore_signal(barrier, inc=1, device_id=place, device_id_type=MESH)

    loads["seg"].wait()
    seg_row = k.in_seg[...].astype(F32)
    seg_cols = jnp.broadcast_to(seg_row, (LANES, ROWS)).T
    k.ext_seg[8:, :] = seg_cols
    k.ext_seg[0:8, :] = jnp.full((8, LANES), -1.0, F32)
    k.seg_send[...] = seg_cols[ROWS - 8 :, :]
    k.seg_out[...] = jnp.broadcast_to(seg_row, (8, ROWS))
    loads["x"].wait()
    k.ext[8:, :] = k.in_x[...].astype(F32)
    k.ext[0:8, :] = jnp.zeros((8, WIDTH), F32)
    loads["conv_w"].wait()
    loads["conv_b"].wait()

    def convolve(count):
        here = k.ext_seg[8 : 8 + count, :]
        same = [k.ext_seg[5 + i : 5 + i + count, :] == here for i in range(3)]
        for lane in range(0, WIDTH, LANES):
            cols = slice(lane, lane + LANES)
            value = jnp.broadcast_to(k.in_conv_b[:, cols], (count, LANES))
            for i in range(4):
                term = k.ext[5 + i : 5 + i + count, cols] * k.in_conv_w[i : i + 1, cols]
                value = value + (jnp.where(same[i], term, 0.0) if i < 3 else term)
            k.conv[0:count, cols] = (value / (1.0 + jnp.exp(-value))).astype(BF16)

    def project(count):
        rows = k.conv[0:count, :]
        k.pay[0:count, 0:RANK] = dot_t(rows, k.in_proj[0:RANK, :]).astype(BF16)
        k.pay[0:count, RANK : RANK + 2 * NST] = dot_t(rows, k.in_proj[RANK:, :]).astype(BF16)

    convolve(ROWS)
    loads["moe"].wait()
    loads["moe_gain"].wait()
    loads["router"].wait()
    moe_rows = k.in_moe[...].astype(F32)
    spread = (iota((LANES, 16), 0) == iota((LANES, 16), 1)).astype(BF16)
    router = dot(spread, k.in_router[...])
    logits_part = dot_t(moe_rows * k.in_moe_gain[...], router, precision=lax.Precision.HIGHEST)
    squares = jnp.sum(moe_rows * moe_rows, axis=1, keepdims=True)
    tail = jnp.where(iota((ROWS, LANES), 1) == 16, squares, logits_part)
    k.pay[:, 640:768] = tail.astype(BF16)
    k.pay[:, 512:640] = jnp.zeros((ROWS, LANES), BF16)
    loads["proj"].wait()
    project(ROWS)

    loads["owner"].wait()
    loads["page"].wait()
    owners = jnp.broadcast_to(k.in_owner[...].astype(F32), (8, 16)).astype(BF16)
    owner_of = dot(owners, (iota((16, ROWS), 0) == iota((16, ROWS), 1) // BLK).astype(BF16))[0:1, :]
    owner_lanes = dot(owners, (iota((16, LANES), 0) == iota((16, LANES), 1)).astype(BF16))[0:1, :]
    owner_rows = jnp.broadcast_to(owner_lanes, (LANES, LANES)).T[0:16, 0:1]
    before = (owner_rows == owner_of) & (iota((16, ROWS), 0) < iota((16, ROWS), 1) // BLK)
    order = jnp.sum(jnp.where(before, 1.0, 0.0), axis=0, keepdims=True)
    slot = jnp.where(order == lax.rem(z, 4).astype(F32), owner_of, -1.0)
    row, col = iota((NG * BLK, ROWS), 0), iota((NG * BLK, ROWS), 1)
    choose = (slot == (row // BLK).astype(F32)) & (row % BLK == col % BLK)
    k.page[...] = k.in_page[...].reshape(ROWS, 2 * HD)
    chosen = dot(jnp.where(choose, 1.0, 0.0).astype(BF16), k.page[...])
    k.outgoing[...] = chosen.astype(BF16).reshape(NG, BLK, 2 * HD)
    loads["pair"].wait()
    k.pair[...] = k.in_pair[...].reshape(ROWS, 2 * HD)
    pl.semaphore_wait(barrier, len(partners))

    behind = {"grp": lax.rem(grp + 1, NG)}
    rim_copy = remote(k.in_x.at[ROWS - 16 : ROWS], k.rim, k.rim_s, k.rim_r, behind)
    rseg_copy = remote(k.seg_send, k.rim_seg, k.rseg_s, k.rseg_r, behind)
    rim_copy.start()
    rseg_copy.start()

    x_copies = {}
    for h in range(2):
        for d, (o, place) in enumerate(zip(others_x, place_x)):
            src = k.pay.at[pl.ds(pl.multiple_of(o * 64, 64), 64), HALF * h : HALF * (h + 1)]
            x_copies[h, d] = remote(src, k.rx.at[h, x], k.x_s.at[h, d], k.x_r.at[h, x], place)
    for (h, d), copy in x_copies.items():
        pl.when(others_x[d] != 0)(copy.start)

    kv_copies = []
    for d in range(1, NG):
        place = {"grp": lax.rem(grp + d, NG)}
        kv_copies.append(remote(k.seg_out, k.seg_all.at[grp], k.sg_s.at[d], k.sg_r.at[grp], place))
        kv_copies.append(remote(k.pair, k.kv_all.at[grp], k.kv_s.at[d], k.kv_r.at[grp], place))
    for i, copy in enumerate(kv_copies):
        pl.when(grp + i // 2 + 1 < NG)(copy.start)

    my_slot, their_slot = lax.rem(z, 4), 3 - lax.rem(z, 4)
    page_copies = []
    for o in range(NG):
        dst = k.out_pages.at[grp, my_slot]
        page_copies.append(remote(k.outgoing.at[o], dst, k.pg_s.at[o], k.pg_r.at[grp], place_p[o]))
    for copy in page_copies:
        copy.start()

    rim_copy.wait()
    rseg_copy.wait()
    k.ext[0:8, :] = k.rim[8:16, :].astype(F32)
    k.ext_seg[0:8, :] = jnp.where(grp == 0, -1.0, k.rim_seg[...])
    convolve(16)
    project(16)
    for (h, d), copy in x_copies.items():
        pl.when(others_x[d] == 0)(copy.start)

    factor = HD**-0.5 * LOG2E

    ones = jnp.ones((ROWS, HD), BF16)

    def attend(key_block, value_block, allowed, first):
        valued = jnp.concatenate([value_block, ones], axis=1)
        for h in range(2):
            scores = dot_t(k.in_q[:, h * HD : (h + 1) * HD], key_block)
            masked = jnp.where(allowed, scores, -HUGE)
            high = jnp.max(masked, axis=1, keepdims=True)
            if first:
                new = high
                weights = jnp.exp2((masked - new) * factor)
                k.accum[h] = dot(weights.astype(BF16), valued)
            else:
                old = k.best[h][:, 0:1]
                new = jnp.maximum(old, high)
                weights = jnp.exp2((masked - new) * factor)
                fade = jnp.exp2((old - new) * factor)
                k.accum[h] = k.accum[h] * fade + dot(weights.astype(BF16), valued)
            k.best[h] = jnp.broadcast_to(new, (ROWS, LANES))

    def earlier(i, carry):
        j = grp - 1 - i
        remote(k.seg_out, k.seg_all.at[j], k.sg_s.at[0], k.sg_r.at[j], place_g[0]).wait_recv()
        remote(k.pair, k.kv_all.at[j], k.kv_s.at[0], k.kv_r.at[j], place_g[0]).wait_recv()
        same = k.seg_all[j, 0:1, :] == k.ext_seg[8:, 0:1]
        attend(k.kv_all[j, :, 0:HD], k.kv_all[j, :, HD:], same, False)
        return carry

    def attend_up_to(first, last):
        lax.fori_loop(jnp.minimum(grp, first), jnp.minimum(grp, last), earlier, 0)

    loads["q"].wait()
    causal = iota((ROWS, ROWS), 1) <= iota((ROWS, ROWS), 0)
    attend(k.pair[:, 0:HD], k.pair[:, HD:], causal & (seg_row == k.ext_seg[8:, 0:1]), True)
    attend_up_to(0, 1)

    z_copies = [
        remote(k.chunk.at[o], k.rz.at[z], k.z_s.at[o], k.z_r.at[z], {"tp": x * NZ + o}) for o in range(NZ)
    ]
    for h in range(2):
        for o in others_x:
            remote(k.rx.at[h, o], k.rx.at[h, o], k.x_s.at[h, 0], k.x_r.at[h, o], place_x[0]).wait_recv()
        summed = k.pay[pl.ds(pl.multiple_of(x * 64, 64), 64), HALF * h : HALF * (h + 1)].astype(F32)
        for o in others_x:
            summed = summed + k.rx[h, o].astype(F32)
        for r in range(4):
            k.chunk[4 * h + r] = summed[16 * r : 16 * r + 16, :].astype(BF16)
        for r in range(4):
            pl.when(z != 4 * h + r)(z_copies[4 * h + r].start)

    loads["z"].wait()
    gate = k.in_z[...].astype(F32)
    k.silu_z[...] = gate / (1.0 + jnp.exp(-gate))

    attend_up_to(1, 2)

    for o in others_z:
        remote(k.chunk.at[0], k.rz.at[o], k.z_s.at[0], k.z_r.at[o], place_z[0]).wait_recv()
    summed = k.chunk[z].astype(F32)
    for o in others_z:
        summed = summed + k.rz[o].astype(F32)
    k.low[x, z] = summed.astype(BF16)
    g_copies = []
    for d, place in enumerate(place_z):
        g_copies.append(remote(k.low.at[x, z], k.low.at[x, z], k.g_s.at[d], k.g_r.at[z], place))
    for copy in g_copies:
        copy.start()
    h_copies = []

    def forward(o):
        for d, place in enumerate(place_x):
            copy = remote(k.low.at[x, o], k.low.at[x, o], k.h_s.at[o, d], k.h_r.at[x, o], place)
            copy.start()
            h_copies.append(copy)

    forward(z)
    for o in others_z:
        remote(k.low.at[x, z], k.low.at[x, o], k.g_s.at[0], k.g_r.at[o], place_z[0]).wait_recv()
        forward(o)

    for o in range(NG):
        remote(k.outgoing.at[0], k.out_pages.at[o, their_slot], k.pg_s.at[0], k.pg_r.at[o], place_p[0]).wait_recv()
    f_copies = []
    for d, place in enumerate(place_q):
        mine = k.out_pages.at[:, their_slot]
        f_copies.append(remote(mine, mine, k.pf_s.at[d], k.pf_r.at[their_slot], place))
    for copy in f_copies:
        copy.start()

    attend_up_to(2, 4)

    for n in ("gain", "dt", "dt_bias", "a_log", "skip", "routing"):
        loads[n].wait()
    for o in others_x:
        for p in range(NZ):
            remote(k.low.at[x, p], k.low.at[o, p], k.h_s.at[0, 0], k.h_r.at[o, p], place_x[0]).wait_recv()
    left = k.low[:, 0:4].reshape(ROWS, HALF).astype(F32)
    right = k.low[:, 4:8].reshape(ROWS, HALF).astype(F32)
    mean = jnp.sum(left * left, axis=1, keepdims=True) + jnp.sum(right[:, :128] * right[:, :128], axis=1, keepdims=True)
    scale = lax.rsqrt(mean / RANK + EPS)
    k.rank[:, 0:HALF] = (left * scale * k.in_gain[:, 0:HALF]).astype(BF16)
    k.rank[:, HALF:RANK] = (right[:, :128] * scale * k.in_gain[:, HALF:RANK]).astype(BF16)
    both = right[:, 128 : 128 + 2 * NST]
    is_b = iota((ROWS, 2 * NST), 1) < NST
    power = both * both
    mean_b = jnp.sum(jnp.where(is_b, power, 0.0), axis=1, keepdims=True) / NST
    mean_c = jnp.sum(jnp.where(is_b, 0.0, power), axis=1, keepdims=True) / NST
    scale = jnp.where(is_b, lax.rsqrt(mean_b + EPS), lax.rsqrt(mean_c + EPS))
    k.bc[...] = (both * scale * k.in_gain[:, RANK : RANK + 2 * NST]).astype(BF16)

    raw = dot(k.rank[...], k.in_dt[...]) + k.in_dt_bias[...]
    step = jnp.maximum(raw, 0.0) + jnp.log(1.0 + jnp.exp(-jnp.abs(raw)))
    k.driven[...] = (step * k.conv[...].astype(F32)).astype(BF16)
    start = jnp.where(k.ext_seg[7 : 7 + ROWS, :] != k.ext_seg[8:, :], HUGE, 0.0)
    for lane in range(0, WIDTH, LANES):
        k.step[:, lane : lane + LANES] = step[:, lane : lane + LANES] + start
    pick = (iota((256, 2 * NST), 0) % NST == iota((256, 2 * NST), 1)).astype(BF16)
    k.b_tiled[...] = dot_t(pick, k.bc[...])
    pick = (iota((2 * NST, 256), 0) == NST + iota((2 * NST, 256), 1) % NST).astype(BF16)
    own = iota((ROWS, 256), 1) // NST == iota((ROWS, 256), 0) % 16
    k.c_blocks[...] = jnp.where(own, dot(k.bc[...], pick), 0.0).astype(BF16)
    rate = jnp.exp(k.in_a_log[...]) * (-LOG2E)

    def scan(b, carry):
        state, left = carry
        mine = iota((256, ROWS), 1) == b * 16 + iota((256, ROWS), 0) // NST
        k.forced[...] = dot(jnp.where(mine, k.b_tiled[...], 0.0).astype(BF16), k.driven[...])
        rows = pl.ds(pl.multiple_of(b * 16, 16), 16)
        steps = k.step[rows, :]
        for t in range(16):
            span = slice(NST * t, NST * (t + 1))
            decay = jnp.exp2(steps[t : t + 1, :] * rate)
            state = decay * state + k.forced[span, :]
            left = decay * left
            k.states[span, :] = state.astype(BF16)
            k.growth[b, span, :] = left.astype(BF16)
        skipped = k.in_skip[...] * k.conv[rows, :].astype(F32)
        k.rows_out[rows, :] = dot(k.c_blocks[rows, :], k.states[...]) + skipped
        return state, left

    begin = (jnp.zeros((NST, WIDTH), F32), jnp.ones((NST, WIDTH), F32))
    state, _ = lax.fori_loop(0, ROWS // 16, scan, begin)
    steps = jnp.sum(k.step[...], axis=0, keepdims=True)
    for i in range(4):
        k.own_end[NST * i : NST * (i + 1), :] = state[:, i * LANES : (i + 1) * LANES].astype(BF16)
    parts = []
    for _ in range(3):
        part = steps.astype(BF16).astype(F32)
        parts += [part[:, i * LANES : (i + 1) * LANES] for i in range(4)]
        steps = steps - part
    k.own_end[64:80, :] = jnp.concatenate(parts + [jnp.zeros((4, LANES), F32)], axis=0).astype(BF16)
    e_copies = []
    for d, place in enumerate(place_g):
        e_copies.append(remote(k.own_end, k.ends.at[grp], k.e_s.at[d], k.e_r.at[grp], place))
    for copy in e_copies:
        copy.start()
    k.ends[grp] = k.own_end[...]

    attend_up_to(4, NG)
    for h in range(2):
        k.out_attn[:, h * HD : (h + 1) * HD] = (k.accum[h, :, 0:HD] / k.accum[h, :, HD:]).astype(BF16)
    stores["attn"].start()
    sums = right[:, 256:384]
    inverse = lax.rsqrt(sums[:, 16:17] / FEATURES + EPS)
    k.out_expert[...] = (k.in_moe[...].astype(F32) * k.in_moe_gain[...] * inverse).astype(BF16)
    logits = (sums * inverse).T
    experts = iota((LANES, ROWS), 0)
    first = jnp.sum(jnp.where(experts == k.in_routing[0:1, :], logits, 0.0), axis=0, keepdims=True)
    second = jnp.sum(jnp.where(experts == k.in_routing[1:2, :], logits, 0.0), axis=0, keepdims=True)
    top = jnp.maximum(first, second)
    first, second = jnp.exp(first - top), jnp.exp(second - top)
    k.out_gate[0:1, :] = first / (first + second)
    k.out_gate[1:2, :] = second / (first + second)
    stores["expert"].start()
    stores["gate"].start()

    for o in others_g:
        remote(k.own_end, k.ends.at[o], k.e_s.at[0], k.e_r.at[o], place_g[0]).wait_recv()
    sums_of = []
    for j in range(NG):
        part = k.ends[j, 64:80, :].astype(F32)
        sums_of.append(part[0:4] + part[4:8] + part[8:12])
    entering = []
    for i in range(4):
        cols = slice(i * LANES, (i + 1) * LANES)
        state = jnp.zeros((NST, LANES), F32)
        mine = state
        for j in range(NG):
            mine = jnp.where(grp == j, state, mine)
            kept = jnp.exp2(sums_of[j][i : i + 1, :] * rate[:, cols])
            state = kept * state + k.ends[j, NST * i : NST * (i + 1), :].astype(F32)
        entering.append(mine)
        for g in range(NG):
            k.own_final[g, 2 * i : 2 * i + 2, :] = state[2 * g : 2 * g + 2, :]
    final_copy = remote(k.own_final.at[grp], k.landed, k.f_s, k.f_r, across)
    final_copy.start()
    entering = jnp.concatenate(entering, axis=1).astype(BF16)

    def finish(b, carry):
        rows = pl.ds(pl.multiple_of(b * 16, 16), 16)
        grown = k.growth[b].reshape(16, NST, WIDTH) * entering[None]
        value = k.rows_out[rows, :] + dot(k.c_blocks[rows, :], grown.reshape(256, WIDTH))
        k.out_mixed[rows, :] = (value * k.silu_z[rows, :]).astype(BF16)
        return carry

    lax.fori_loop(0, ROWS // 16, finish, 0)
    stores["mixed"].start()

    final_copy.wait()
    for i in range(4):
        k.out_final[:, i * LANES : (i + 1) * LANES] = k.landed[2 * i : 2 * i + 2, :]
    stores["final"].start()
    for o in others_q:
        theirs = k.out_pages.at[:, 3 - lax.rem(o, 4)]
        remote(theirs, theirs, k.pf_s.at[0], k.pf_r.at[3 - lax.rem(o, 4)], place_q[0]).wait_recv()
    for copy in list(x_copies.values()) + g_copies + h_copies + page_copies + f_copies + e_copies:
        copy.wait_send()
    for o in range(NZ):
        pl.when(z != o)(z_copies[o].wait_send)
    for i, copy in enumerate(kv_copies):
        pl.when(grp + i // 2 + 1 < NG)(copy.wait_send)
    for store in stores.values():
        store.wait()


def hand_out(*refs):
    count = len(OUTPUTS)
    source, target, stage = refs[:count], refs[count : 2 * count], refs[2 * count : 3 * count]
    read, write = refs[3 * count :]
    inward = [pltpu.make_async_copy(source[i], stage[i], read.at[i]) for i in range(count)]
    outward = [pltpu.make_async_copy(stage[i], target[i], write.at[i]) for i in range(count)]
    for copy in inward:
        copy.start()
    for i in range(count):
        inward[i].wait()
        outward[i].start()
    for copy in outward:
        copy.wait()


def local(
    mamba_x, mamba_z, conv_weight, conv_bias, x_proj, norm_gain, dt_proj, dt_bias, a_log, d_skip,
    segment_ids, queries, keys_values, kv_owner, moe_in, moe_gain, router, routing,
):
    inputs = dict(
        x=mamba_x, seg=segment_ids, conv_w=conv_weight, conv_b=conv_bias.reshape(1, -1), proj=x_proj.T,
        owner=kv_owner.reshape(1, -1), keys_values=keys_values, moe=moe_in, moe_gain=moe_gain.reshape(1, -1), router=router.T, q=queries,
        z=mamba_z, gain=norm_gain.reshape(1, -1), dt=dt_proj, dt_bias=dt_bias.reshape(1, -1), a_log=a_log,
        skip=d_skip.reshape(1, -1), routing=routing.T,
    )
    shapes = tuple(jax.ShapeDtypeStruct(s, t) for _, s, t in OUTPUTS)
    results = pl.pallas_call(
        main_kernel,
        out_shape=shapes,
        in_specs=[ANY] * len(OPERANDS),
        out_specs=tuple([ANY] * len(OUTPUTS)),
        scratch_shapes=[pltpu.VMEM(s, t) for _, s, t in SCRATCH]
        + [pltpu.VMEM(s, t) for _, s, t in INPUTS]
        + [pltpu.VMEM(s, t) for n, s, t in OUTPUTS if n != "pages"]
        + [DMA(s) if s else DMA for _, s in SEMS],
        compiler_params=pltpu.CompilerParams(
            vmem_limit_bytes=62 << 20, collective_id=0, has_side_effects=True
        ),
        name="span",
    )(*[inputs[n] for n in OPERANDS])
    mixed, final, attn, pages, expert, gates = pl.pallas_call(
        hand_out,
        out_shape=shapes,
        in_specs=[ANY] * len(OUTPUTS),
        out_specs=tuple([ANY] * len(OUTPUTS)),
        scratch_shapes=[pltpu.VMEM(s, t) for _, s, t in OUTPUTS] + [DMA((len(OUTPUTS),))] * 2,
        compiler_params=pltpu.CompilerParams(vmem_limit_bytes=62 << 20),
        name="results",
    )(*results)
    return (mixed, final[None], attn, pages.reshape(1, 1, 1, NG * SLOTS, BLK, 2 * HD), expert, gates.T)


def solution(mesh):
    placed = (
        P(("sect", "grp"), "tp"),
        P(("sect", "grp"), "tp"),
        P(None, "tp"),
        P("tp"),
        P("tp", None),
        P(),
        P(None, "tp"),
        P("tp"),
        P(None, "tp"),
        P("tp"),
        P("sect", "grp"),
        P(("sect", "grp"), "tp"),
        P(("sect", "grp"), None, None),
        P("sect", "grp", None),
        P(("sect", "grp"), "tp"),
        P("tp"),
        P("tp", None),
        P(("sect", "grp"), None),
    )
    return jax.shard_map(
        local,
        mesh=mesh,
        in_specs=placed,
        out_specs=(
            P(("sect", "grp"), "tp"),
            P("sect", "grp", "tp"),
            P(("sect", "grp"), "tp"),
            P("sect", "grp", "tp", None, None, None),
            P(("sect", "grp"), "tp"),
            P(("sect", "grp"), None),
        ),
        check_vma=False,
    )
```

profile of v0, /device:TPU:1, one launch (start us, length us, event | category | flops | bytes accessed | tf_op | source)
XLA Modules:
  0.0 64.2 jit_solution(11586186756139644018)
XLA Ops:
  0.6 0.0 copy-start
  0.6 0.7 %copy-done = f32[544]{0:T(1024)S(1)} copy-done((f32[544]{0:T(1024)S(1)}, f32[544]{0:T(1024)}, u32[]{:S(2)}) %copy-start) | copy-done | bytes 2200
  1.3 0.6 reshape.36.refs_11_
  1.9 60.4 %span.1 = (bf16[256,512]{1,0:T(8,128)(2,1)}, f32[2,512]{1,0:T(2,128)}, bf16[256,256]{1,0:T(8,128)(2,1)}, bf16[8,4,16,256]{3,2,1,0:T(8,128)(2,1)}, bf16[256,256]{1,0:T(8,128)(2,1)}, /*index=5*/f32[2,256]{1,0:T(2,128)}) custom-call(bf16[256,512]{1,0:T(8,128)(2,1)} %refs_0_.1, s32[1,256]{1,0:T(1,128)} %refs_1_.1, f32[4,512]{1,0:T(4,128)} %refs_2_.1, ...), custom_call_target="tpu_custom_call" | custom-call | tf_op jit(solution)/shard_map/span/pallas_call | solution.py:526
  62.3 1.9 %results.1 = (bf16[256,512]{1,0:T(8,128)(2,1)}, f32[2,512]{1,0:T(2,128)}, bf16[256,256]{1,0:T(8,128)(2,1)}, bf16[8,4,16,256]{3,2,1,0:T(8,128)(2,1)}, bf16[256,256]{1,0:T(8,128)(2,1)}, /*index=5*/f32[2,256]{1,0:T(2,128)}) custom-call(bf16[256,512]{1,0:T(8,128)(2,1)} %get-tuple-element.18.refs_0_, f32[2,512]{1,0:T(2,128)} %get-tuple-element.19.refs_1_, ...), custom_call_target="tpu_custom_call" | custom-call | tf_op jit(solution)/shard_map/results/pallas_call | solution.py:540
Async XLA Ops:
  0.6 0.7 %copy-start = (f32[544]{0:T(1024)S(1)}, f32[544]{0:T(1024)}, u32[]{:S(2)}) copy-start(f32[544]{0:T(1024)} %param.23) | copy-start | bytes 6532
where the time goes:
time: 64.4 us; the launch traced here: 64.2 us
  Pallas kernels  62.3 us (97%)
  local copies, waits for them, and re-layouts  1.26 us (2%)
  between operations  0.65 us (1%)
    pallas_call x1, Pallas kernels, local(): pl.pallas_call(main_kernel, out_shape=shapes, in_specs=[ANY] * len(OPERAN...  60.4 us
    pallas_call x1, Pallas kernels, local(): pl.pallas_call(hand_out, out_shape=shapes, in_specs=[ANY] * len(OUTPUTS),...  1.95 us

commit v1 on v0

--- a/solution.py
+++ b/solution.py
@@ -62,7 +62,7 @@
     ("router", (16, 256), BF16),
     ("q", (ROWS, 2 * HD), BF16),
     ("z", (ROWS, WIDTH), BF16),
-    ("gain", (1, RANK + 2 * NST), F32),
+    ("gain", (RANK + 2 * NST,), F32),
     ("dt", (RANK, WIDTH), BF16),
     ("dt_bias", (1, WIDTH), F32),
     ("a_log", (NST, WIDTH), F32),
@@ -102,13 +102,11 @@
     ("rank", (ROWS, RANK), BF16),
     ("bc", (ROWS, 2 * NST), BF16),
     ("step", (ROWS, WIDTH), F32),
-    ("driven", (ROWS, WIDTH), BF16),
-    ("b_tiled", (256, ROWS), F32),
+    ("driven", (ROWS, WIDTH), F32),
+    ("b_cols", (16, NST, LANES), F32),
     ("c_blocks", (ROWS, 256), BF16),
-    ("forced", (256, WIDTH), F32),
-    ("states", (256, WIDTH), BF16),
+    ("states", (16, 256, WIDTH), BF16),
     ("growth", (16, 256, WIDTH), BF16),
-    ("rows_out", (ROWS, WIDTH), F32),
     ("ends", (NG, 80, LANES), BF16),
     ("own_end", (80, LANES), BF16),
     ("own_final", (NG, 8, LANES), F32),
@@ -118,6 +116,7 @@
     ("load", (len(INPUTS),)), ("store", (len(OUTPUTS),)),
     ("rim_s", ()), ("rim_r", ()), ("rseg_s", ()), ("rseg_r", ()),
     ("kv_s", (NG,)), ("kv_r", (NG,)), ("sg_s", (NG,)), ("sg_r", (NG,)),
+    ("sw_s", (NG,)), ("sw_r", (NG,)),
     ("pg_s", (NG,)), ("pg_r", (NG,)), ("pf_s", (4,)), ("pf_r", (4,)),
     ("x_s", (2, NX)), ("x_r", (2, NX)), ("z_s", (NZ,)), ("z_r", (NZ,)),
     ("g_s", (NZ,)), ("g_r", (NZ,)), ("h_s", (NZ, NX)), ("h_r", (NX, NZ)),
@@ -139,6 +138,9 @@
     k.out_pages = k.hbm_out_pages
     sect, tp, grp = lax.axis_index("sect"), lax.axis_index("tp"), lax.axis_index("grp")
     x, z = tp // NZ, tp % NZ
+    chip, core = grp // 2, grp % 2
+    twin = {"grp": grp + 1 - 2 * core}
+    half_rows = pl.ds(pl.multiple_of(128 * core, 128), 128)
     heads = {"pair": tp // 4, "page": 2 * x + (NZ - 1 - z) // 4}
     loads = {}
     for i, (n, _, _) in enumerate(INPUTS):
@@ -248,10 +250,17 @@
     kv_copies = []
     for d in range(1, NG):
         place = {"grp": lax.rem(grp + d, NG)}
-        kv_copies.append(remote(k.seg_out, k.seg_all.at[grp], k.sg_s.at[d], k.sg_r.at[grp], place))
-        kv_copies.append(remote(k.pair, k.kv_all.at[grp], k.kv_s.at[d], k.kv_r.at[grp], place))
-    for i, copy in enumerate(kv_copies):
-        pl.when(grp + i // 2 + 1 < NG)(copy.start)
+        copy = remote(k.seg_out, k.seg_all.at[grp], k.sg_s.at[d], k.sg_r.at[grp], place)
+        kv_copies.append((grp + d < NG, copy))
+    for d in range(1, NG // 2):
+        for half in range(2):
+            rows = slice(128 * half, 128 * half + 128)
+            place = {"grp": 2 * lax.rem(chip + d, NG // 2) + half}
+            copy = remote(k.pair.at[rows], k.kv_all.at[grp, rows], k.kv_s.at[2 * d + half], k.kv_r.at[grp], place)
+            kv_copies.append((chip + d < NG // 2, copy))
+    kv_copies.append((core == 0, remote(k.pair, k.kv_all.at[grp], k.kv_s.at[0], k.kv_r.at[grp], twin)))
+    for here, copy in kv_copies:
+        pl.when(here)(copy.start)
 
     my_slot, their_slot = lax.rem(z, 4), 3 - lax.rem(z, 4)
     page_copies = []
@@ -292,21 +301,33 @@
                 k.accum[h] = k.accum[h] * fade + dot(weights.astype(BF16), valued)
             k.best[h] = jnp.broadcast_to(new, (ROWS, LANES))
 
-    def earlier(i, carry):
-        j = grp - 1 - i
+    def attend_block(j):
         remote(k.seg_out, k.seg_all.at[j], k.sg_s.at[0], k.sg_r.at[j], place_g[0]).wait_recv()
-        remote(k.pair, k.kv_all.at[j], k.kv_s.at[0], k.kv_r.at[j], place_g[0]).wait_recv()
         same = k.seg_all[j, 0:1, :] == k.ext_seg[8:, 0:1]
         attend(k.kv_all[j, :, 0:HD], k.kv_all[j, :, HD:], same, False)
+
+    def swap(i):
+        block = k.kv_all.at[2 * chip - 1 - i, half_rows]
+        return remote(block, block, k.sw_s.at[i], k.sw_r.at[i], twin)
+
+    def swap_start(i, carry):
+        block = k.kv_all.at[2 * chip - 1 - i, half_rows]
+        remote(block, block, k.sw_s.at[i], k.kv_r.at[2 * chip - 1 - i], twin).wait_recv()
+        swap(i).start()
         return carry
 
-    def attend_up_to(first, last):
-        lax.fori_loop(jnp.minimum(grp, first), jnp.minimum(grp, last), earlier, 0)
+    def swap_end(i, carry):
+        swap(i).wait_send()
+        return carry
+
+    def earlier(i, carry):
+        swap(i).wait_recv()
+        attend_block(2 * chip - 1 - i)
+        return carry
 
     loads["q"].wait()
     causal = iota((ROWS, ROWS), 1) <= iota((ROWS, ROWS), 0)
     attend(k.pair[:, 0:HD], k.pair[:, HD:], causal & (seg_row == k.ext_seg[8:, 0:1]), True)
-    attend_up_to(0, 1)
 
     z_copies = [
         remote(k.chunk.at[o], k.rz.at[z], k.z_s.at[o], k.z_r.at[z], {"tp": x * NZ + o}) for o in range(NZ)
@@ -326,7 +347,11 @@
     gate = k.in_z[...].astype(F32)
     k.silu_z[...] = gate / (1.0 + jnp.exp(-gate))
 
-    attend_up_to(1, 2)
+
+    @pl.when(core == 1)
+    def _():
+        remote(k.pair, k.kv_all.at[grp - 1], k.kv_s.at[0], k.kv_r.at[grp - 1], twin).wait_recv()
+        attend_block(grp - 1)
 
     for o in others_z:
         remote(k.chunk.at[0], k.rz.at[o], k.z_s.at[0], k.z_r.at[o], place_z[0]).wait_recv()
@@ -352,6 +377,8 @@
         remote(k.low.at[x, z], k.low.at[x, o], k.g_s.at[0], k.g_r.at[o], place_z[0]).wait_recv()
         forward(o)
 
+    lax.fori_loop(0, 2 * chip, swap_start, 0)
+
     for o in range(NG):
         remote(k.outgoing.at[0], k.out_pages.at[o, their_slot], k.pg_s.at[0], k.pg_r.at[o], place_p[0]).wait_recv()
     f_copies = []
@@ -361,35 +388,38 @@
     for copy in f_copies:
         copy.start()
 
-    attend_up_to(2, 4)
+    lax.fori_loop(0, jnp.minimum(2 * chip, 3), earlier, 0)
 
     for n in ("gain", "dt", "dt_bias", "a_log", "skip", "routing"):
         loads[n].wait()
     for o in others_x:
         for p in range(NZ):
             remote(k.low.at[x, p], k.low.at[o, p], k.h_s.at[0, 0], k.h_r.at[o, p], place_x[0]).wait_recv()
+    gain = k.in_gain[...].reshape(1, RANK + 2 * NST)
     left = k.low[:, 0:4].reshape(ROWS, HALF).astype(F32)
     right = k.low[:, 4:8].reshape(ROWS, HALF).astype(F32)
     mean = jnp.sum(left * left, axis=1, keepdims=True) + jnp.sum(right[:, :128] * right[:, :128], axis=1, keepdims=True)
     scale = lax.rsqrt(mean / RANK + EPS)
-    k.rank[:, 0:HALF] = (left * scale * k.in_gain[:, 0:HALF]).astype(BF16)
-    k.rank[:, HALF:RANK] = (right[:, :128] * scale * k.in_gain[:, HALF:RANK]).astype(BF16)
+    k.rank[:, 0:HALF] = (left * scale * gain[:, 0:HALF]).astype(BF16)
+    k.rank[:, HALF:RANK] = (right[:, :128] * scale * gain[:, HALF:RANK]).astype(BF16)
     both = right[:, 128 : 128 + 2 * NST]
     is_b = iota((ROWS, 2 * NST), 1) < NST
     power = both * both
     mean_b = jnp.sum(jnp.where(is_b, power, 0.0), axis=1, keepdims=True) / NST
     mean_c = jnp.sum(jnp.where(is_b, 0.0, power), axis=1, keepdims=True) / NST
     scale = jnp.where(is_b, lax.rsqrt(mean_b + EPS), lax.rsqrt(mean_c + EPS))
-    k.bc[...] = (both * scale * k.in_gain[:, RANK : RANK + 2 * NST]).astype(BF16)
+    k.bc[...] = (both * scale * gain[:, RANK : RANK + 2 * NST]).astype(BF16)
 
     raw = dot(k.rank[...], k.in_dt[...]) + k.in_dt_bias[...]
     step = jnp.maximum(raw, 0.0) + jnp.log(1.0 + jnp.exp(-jnp.abs(raw)))
-    k.driven[...] = (step * k.conv[...].astype(F32)).astype(BF16)
+    k.driven[...] = step * k.conv[...].astype(F32)
     start = jnp.where(k.ext_seg[7 : 7 + ROWS, :] != k.ext_seg[8:, :], HUGE, 0.0)
     for lane in range(0, WIDTH, LANES):
         k.step[:, lane : lane + LANES] = step[:, lane : lane + LANES] + start
-    pick = (iota((256, 2 * NST), 0) % NST == iota((256, 2 * NST), 1)).astype(BF16)
-    k.b_tiled[...] = dot_t(pick, k.bc[...])
+    pick = (iota((NST, 2 * NST), 0) == iota((NST, 2 * NST), 1)).astype(BF16)
+    b_all = dot_t(pick, k.bc[...])
+    for b in range(16):
+        k.b_cols[b, :, 0:16] = b_all[:, 16 * b : 16 * b + 16]
     pick = (iota((2 * NST, 256), 0) == NST + iota((2 * NST, 256), 1) % NST).astype(BF16)
     own = iota((ROWS, 256), 1) // NST == iota((ROWS, 256), 0) % 16
     k.c_blocks[...] = jnp.where(own, dot(k.bc[...], pick), 0.0).astype(BF16)
@@ -397,19 +427,15 @@
 
     def scan(b, carry):
         state, left = carry
-        mine = iota((256, ROWS), 1) == b * 16 + iota((256, ROWS), 0) // NST
-        k.forced[...] = dot(jnp.where(mine, k.b_tiled[...], 0.0).astype(BF16), k.driven[...])
         rows = pl.ds(pl.multiple_of(b * 16, 16), 16)
-        steps = k.step[rows, :]
+        steps, driven, b_cols = k.step[rows, :], k.driven[rows, :], k.b_cols[b]
         for t in range(16):
             span = slice(NST * t, NST * (t + 1))
             decay = jnp.exp2(steps[t : t + 1, :] * rate)
-            state = decay * state + k.forced[span, :]
+            state = decay * state + b_cols[:, t : t + 1] * driven[t : t + 1, :]
             left = decay * left
-            k.states[span, :] = state.astype(BF16)
+            k.states[b, span, :] = state.astype(BF16)
             k.growth[b, span, :] = left.astype(BF16)
-        skipped = k.in_skip[...] * k.conv[rows, :].astype(F32)
-        k.rows_out[rows, :] = dot(k.c_blocks[rows, :], k.states[...]) + skipped
         return state, left
 
     begin = (jnp.zeros((NST, WIDTH), F32), jnp.ones((NST, WIDTH), F32))
@@ -430,7 +456,7 @@
         copy.start()
     k.ends[grp] = k.own_end[...]
 
-    attend_up_to(4, NG)
+    lax.fori_loop(jnp.minimum(2 * chip, 3), 2 * chip, earlier, 0)
     for h in range(2):
         k.out_attn[:, h * HD : (h + 1) * HD] = (k.accum[h, :, 0:HD] / k.accum[h, :, HD:]).astype(BF16)
     stores["attn"].start()
@@ -472,12 +498,13 @@
 
     def finish(b, carry):
         rows = pl.ds(pl.multiple_of(b * 16, 16), 16)
-        grown = k.growth[b].reshape(16, NST, WIDTH) * entering[None]
-        value = k.rows_out[rows, :] + dot(k.c_blocks[rows, :], grown.reshape(256, WIDTH))
+        grown = k.growth[b].reshape(16, NST, WIDTH) * entering[None] + k.states[b].reshape(16, NST, WIDTH)
+        value = dot(k.c_blocks[rows, :], grown.reshape(256, WIDTH))
+        value = value + k.in_skip[...] * k.conv[rows, :].astype(F32)
         k.out_mixed[rows, :] = (value * k.silu_z[rows, :]).astype(BF16)
         return carry
 
-    lax.fori_loop(0, ROWS // 16, finish, 0)
+    lax.fori_loop(0, ROWS // 16, finish, 0, unroll=4)
     stores["mixed"].start()
 
     final_copy.wait()
@@ -491,8 +518,9 @@
         copy.wait_send()
     for o in range(NZ):
         pl.when(z != o)(z_copies[o].wait_send)
-    for i, copy in enumerate(kv_copies):
-        pl.when(grp + i // 2 + 1 < NG)(copy.wait_send)
+    lax.fori_loop(0, 2 * chip, swap_end, 0)
+    for here, copy in kv_copies:
+        pl.when(here)(copy.wait_send)
     for store in stores.values():
         store.wait()
 
@@ -519,7 +547,7 @@
     inputs = dict(
         x=mamba_x, seg=segment_ids, conv_w=conv_weight, conv_b=conv_bias.reshape(1, -1), proj=x_proj.T,
         owner=kv_owner.reshape(1, -1), keys_values=keys_values, moe=moe_in, moe_gain=moe_gain.reshape(1, -1), router=router.T, q=queries,
-        z=mamba_z, gain=norm_gain.reshape(1, -1), dt=dt_proj, dt_bias=dt_bias.reshape(1, -1), a_log=a_log,
+        z=mamba_z, gain=norm_gain, dt=dt_proj, dt_bias=dt_bias.reshape(1, -1), a_log=a_log,
         skip=d_skip.reshape(1, -1), routing=routing.T,
     )
     shapes = tuple(jax.ShapeDtypeStruct(s, t) for _, s, t in OUTPUTS)

time: 64.4 us -> 60.8 us (0.944)
  Pallas kernels: 62.3 us -> 60 us
  local copies, waits for them, and re-layouts: 1.26 us -> 0 us
    pallas_call x1, Pallas kernels: 60.4 us -> 58 us  [local(): pl.pallas_call(main_kernel, out_shape=shapes, in_specs=[ANY] * len(OPERAN...]
    unnamed x2 -> x0, local copies, waits for them, and re-layouts: 0.68 us -> none
where the time goes in v1:
time: 60.8 us; the launch traced here: 60.6 us
  Pallas kernels  60 us (99%)
  between operations  0.65 us (1%)
    pallas_call x1, Pallas kernels, local(): pl.pallas_call(main_kernel, out_shape=shapes, in_specs=[ANY] * len(OPERAN...  58 us
    pallas_call x1, Pallas kernels, local(): pl.pallas_call(hand_out, out_shape=shapes, in_specs=[ANY] * len(OUTPUTS),...  1.95 us

profile of v1, /device:TPU:1, one launch (start us, length us, event | category | flops | bytes accessed | tf_op | source)
XLA Modules:
  0.0 60.6 jit_solution(15923782470686656617)
XLA Ops:
  0.6 58.0 %span.1 = (bf16[256,512]{1,0:T(8,128)(2,1)}, f32[2,512]{1,0:T(2,128)}, bf16[256,256]{1,0:T(8,128)(2,1)}, bf16[8,4,16,256]{3,2,1,0:T(8,128)(2,1)}, bf16[256,256]{1,0:T(8,128)(2,1)}, /*index=5*/f32[2,256]{1,0:T(2,128)}) custom-call(bf16[256,512]{1,0:T(8,128)(2,1)} %refs_0_.1, s32[1,256]{1,0:T(1,128)} %refs_1_.1, f32[4,512]{1,0:T(4,128)} %refs_2_.1, ...), custom_call_target="tpu_custom_call" | custom-call | tf_op jit(solution)/shard_map/span/pallas_call | solution.py:554
  58.7 1.9 %results.1 = (bf16[256,512]{1,0:T(8,128)(2,1)}, f32[2,512]{1,0:T(2,128)}, bf16[256,256]{1,0:T(8,128)(2,1)}, bf16[8,4,16,256]{3,2,1,0:T(8,128)(2,1)}, bf16[256,256]{1,0:T(8,128)(2,1)}, /*index=5*/f32[2,256]{1,0:T(2,128)}) custom-call(bf16[256,512]{1,0:T(8,128)(2,1)} %get-tuple-element.18.refs_0_, f32[2,512]{1,0:T(2,128)} %get-tuple-element.19.refs_1_, ...), custom_call_target="tpu_custom_call" | custom-call | tf_op jit(solution)/shard_map/results/pallas_call | solution.py:568

commit v2 on v1

--- a/solution.py
+++ b/solution.py
@@ -18,11 +18,13 @@
 BLK = 16
 LANES = 128
 NX, NZ, NG = 4, 8, 8
-PAY = 768
-HALF = PAY // 2
+PAY = 640
+CUTS = (0, 384, 640)
+WIDE = (384, 256)
 SLOTS = 4
 FEATURES = 8192
 EPS = 1e-06
+SQUARES = 2 * NST + 16
 LOG2E = 1.4426950408889634
 HUGE = 1e30
 VMEM = pl.BlockSpec(memory_space=pltpu.VMEM)
@@ -91,10 +93,14 @@
     ("ext_seg", (8 + ROWS, LANES), F32),
     ("conv", (ROWS, WIDTH), BF16),
     ("pay", (ROWS, PAY), BF16),
-    ("rx", (2, NX, 64, HALF), BF16),
-    ("chunk", (NZ, 16, HALF), BF16),
-    ("rz", (NZ, 16, HALF), BF16),
-    ("low", (NX, NZ, 16, HALF), BF16),
+    ("rx0", (NX, 64, WIDE[0]), BF16),
+    ("rx1", (NX, 64, WIDE[1]), BF16),
+    ("chunk0", (4, 16, WIDE[0]), BF16),
+    ("chunk1", (4, 16, WIDE[1]), BF16),
+    ("rz0", (NZ, 16, WIDE[0]), BF16),
+    ("rz1", (NZ, 16, WIDE[1]), BF16),
+    ("low0", (NX, 4, 16, WIDE[0]), BF16),
+    ("low1", (NX, 4, 16, WIDE[1]), BF16),
     ("outgoing", (NG, BLK, 2 * HD), BF16),
     ("best", (2, ROWS, LANES), F32),
     ("accum", (2, ROWS, 2 * HD), F32),
@@ -171,49 +177,37 @@
     for place in partners:
         pl.semaphore_signal(barrier, inc=1, device_id=place, device_id_type=MESH)
 
+    loads["x"].wait()
     loads["seg"].wait()
     seg_row = k.in_seg[...].astype(F32)
     seg_cols = jnp.broadcast_to(seg_row, (LANES, ROWS)).T
     k.ext_seg[8:, :] = seg_cols
-    k.ext_seg[0:8, :] = jnp.full((8, LANES), -1.0, F32)
     k.seg_send[...] = seg_cols[ROWS - 8 :, :]
     k.seg_out[...] = jnp.broadcast_to(seg_row, (8, ROWS))
-    loads["x"].wait()
-    k.ext[8:, :] = k.in_x[...].astype(F32)
-    k.ext[0:8, :] = jnp.zeros((8, WIDTH), F32)
-    loads["conv_w"].wait()
-    loads["conv_b"].wait()
-
-    def convolve(count):
-        here = k.ext_seg[8 : 8 + count, :]
-        same = [k.ext_seg[5 + i : 5 + i + count, :] == here for i in range(3)]
-        for lane in range(0, WIDTH, LANES):
-            cols = slice(lane, lane + LANES)
-            value = jnp.broadcast_to(k.in_conv_b[:, cols], (count, LANES))
-            for i in range(4):
-                term = k.ext[5 + i : 5 + i + count, cols] * k.in_conv_w[i : i + 1, cols]
-                value = value + (jnp.where(same[i], term, 0.0) if i < 3 else term)
-            k.conv[0:count, cols] = (value / (1.0 + jnp.exp(-value))).astype(BF16)
-
-    def project(count):
-        rows = k.conv[0:count, :]
-        k.pay[0:count, 0:RANK] = dot_t(rows, k.in_proj[0:RANK, :]).astype(BF16)
-        k.pay[0:count, RANK : RANK + 2 * NST] = dot_t(rows, k.in_proj[RANK:, :]).astype(BF16)
-
-    convolve(ROWS)
-    loads["moe"].wait()
-    loads["moe_gain"].wait()
-    loads["router"].wait()
-    moe_rows = k.in_moe[...].astype(F32)
-    spread = (iota((LANES, 16), 0) == iota((LANES, 16), 1)).astype(BF16)
-    router = dot(spread, k.in_router[...])
-    logits_part = dot_t(moe_rows * k.in_moe_gain[...], router, precision=lax.Precision.HIGHEST)
-    squares = jnp.sum(moe_rows * moe_rows, axis=1, keepdims=True)
-    tail = jnp.where(iota((ROWS, LANES), 1) == 16, squares, logits_part)
-    k.pay[:, 640:768] = tail.astype(BF16)
-    k.pay[:, 512:640] = jnp.zeros((ROWS, LANES), BF16)
-    loads["proj"].wait()
-    project(ROWS)
+    pl.semaphore_wait(barrier, len(partners))
+
+    behind = {"grp": lax.rem(grp + 1, NG)}
+    rim_copy = remote(k.in_x.at[ROWS - 16 : ROWS], k.rim, k.rim_s, k.rim_r, behind)
+    rseg_copy = remote(k.seg_send, k.rim_seg, k.rseg_s, k.rseg_r, behind)
+    rim_copy.start()
+    rseg_copy.start()
+
+    loads["pair"].wait()
+    k.pair[...] = k.in_pair[...].reshape(ROWS, 2 * HD)
+    kv_copies = []
+    for d in range(1, NG):
+        place = {"grp": lax.rem(grp + d, NG)}
+        copy = remote(k.seg_out, k.seg_all.at[grp], k.sg_s.at[d], k.sg_r.at[grp], place)
+        kv_copies.append((grp + d < NG, copy))
+    for d in range(1, NG // 2):
+        for half in range(2):
+            rows = slice(128 * half, 128 * half + 128)
+            place = {"grp": 2 * lax.rem(chip + d, NG // 2) + half}
+            copy = remote(k.pair.at[rows], k.kv_all.at[grp, rows], k.kv_s.at[2 * d + half], k.kv_r.at[grp], place)
+            kv_copies.append((chip + d < NG // 2, copy))
+    kv_copies.append((core == 0, remote(k.pair, k.kv_all.at[grp], k.kv_s.at[0], k.kv_r.at[grp], twin)))
+    for here, copy in kv_copies:
+        pl.when(here)(copy.start)
 
     loads["owner"].wait()
     loads["page"].wait()
@@ -229,39 +223,6 @@
     k.page[...] = k.in_page[...].reshape(ROWS, 2 * HD)
     chosen = dot(jnp.where(choose, 1.0, 0.0).astype(BF16), k.page[...])
     k.outgoing[...] = chosen.astype(BF16).reshape(NG, BLK, 2 * HD)
-    loads["pair"].wait()
-    k.pair[...] = k.in_pair[...].reshape(ROWS, 2 * HD)
-    pl.semaphore_wait(barrier, len(partners))
-
-    behind = {"grp": lax.rem(grp + 1, NG)}
-    rim_copy = remote(k.in_x.at[ROWS - 16 : ROWS], k.rim, k.rim_s, k.rim_r, behind)
-    rseg_copy = remote(k.seg_send, k.rim_seg, k.rseg_s, k.rseg_r, behind)
-    rim_copy.start()
-    rseg_copy.start()
-
-    x_copies = {}
-    for h in range(2):
-        for d, (o, place) in enumerate(zip(others_x, place_x)):
-            src = k.pay.at[pl.ds(pl.multiple_of(o * 64, 64), 64), HALF * h : HALF * (h + 1)]
-            x_copies[h, d] = remote(src, k.rx.at[h, x], k.x_s.at[h, d], k.x_r.at[h, x], place)
-    for (h, d), copy in x_copies.items():
-        pl.when(others_x[d] != 0)(copy.start)
-
-    kv_copies = []
-    for d in range(1, NG):
-        place = {"grp": lax.rem(grp + d, NG)}
-        copy = remote(k.seg_out, k.seg_all.at[grp], k.sg_s.at[d], k.sg_r.at[grp], place)
-        kv_copies.append((grp + d < NG, copy))
-    for d in range(1, NG // 2):
-        for half in range(2):
-            rows = slice(128 * half, 128 * half + 128)
-            place = {"grp": 2 * lax.rem(chip + d, NG // 2) + half}
-            copy = remote(k.pair.at[rows], k.kv_all.at[grp, rows], k.kv_s.at[2 * d + half], k.kv_r.at[grp], place)
-            kv_copies.append((chip + d < NG // 2, copy))
-    kv_copies.append((core == 0, remote(k.pair, k.kv_all.at[grp], k.kv_s.at[0], k.kv_r.at[grp], twin)))
-    for here, copy in kv_copies:
-        pl.when(here)(copy.start)
-
     my_slot, their_slot = lax.rem(z, 4), 3 - lax.rem(z, 4)
     page_copies = []
     for o in range(NG):
@@ -270,14 +231,50 @@
     for copy in page_copies:
         copy.start()
 
+    loads["moe"].wait()
+    loads["moe_gain"].wait()
+    loads["router"].wait()
+    moe_rows = k.in_moe[...].astype(F32)
+    spread = (iota((LANES, 16), 0) == iota((LANES, 16), 1) + 2 * NST).astype(BF16)
+    router = dot(spread, k.in_router[...])
+    logits_part = dot_t(moe_rows * k.in_moe_gain[...], router, precision=lax.Precision.HIGHEST)
+    squares = jnp.sum(moe_rows * moe_rows, axis=1, keepdims=True)
+    tail = jnp.where(iota((ROWS, LANES), 1) == SQUARES, squares, logits_part)
+
+    k.ext[8:, :] = k.in_x[...].astype(F32)
+    loads["conv_w"].wait()
+    loads["conv_b"].wait()
+    loads["proj"].wait()
     rim_copy.wait()
     rseg_copy.wait()
     k.ext[0:8, :] = k.rim[8:16, :].astype(F32)
     k.ext_seg[0:8, :] = jnp.where(grp == 0, -1.0, k.rim_seg[...])
-    convolve(16)
-    project(16)
-    for (h, d), copy in x_copies.items():
-        pl.when(others_x[d] == 0)(copy.start)
+    here = k.ext_seg[8:, :]
+    same = [k.ext_seg[5 + i : 5 + i + ROWS, :] == here for i in range(3)]
+    for lane in range(0, WIDTH, LANES):
+        cols = slice(lane, lane + LANES)
+        value = jnp.broadcast_to(k.in_conv_b[:, cols], (ROWS, LANES))
+        for i in range(4):
+            term = k.ext[5 + i : 5 + i + ROWS, cols] * k.in_conv_w[i : i + 1, cols]
+            value = value + (jnp.where(same[i], term, 0.0) if i < 3 else term)
+        k.conv[:, cols] = (value / (1.0 + jnp.exp(-value))).astype(BF16)
+    conv = k.conv[...]
+
+    rx, chunk, rz, low = (k.rx0, k.rx1), (k.chunk0, k.chunk1), (k.rz0, k.rz1), (k.low0, k.low1)
+    x_copies = []
+    for h in range(2):
+        if h == 0:
+            k.pay[:, 0:384] = dot_t(conv, k.in_proj[0:384, :]).astype(BF16)
+        else:
+            k.pay[:, 384:RANK] = dot_t(conv, k.in_proj[384:RANK, :]).astype(BF16)
+            spread = (iota((LANES, 2 * NST), 0) == iota((LANES, 2 * NST), 1)).astype(BF16)
+            last = dot(spread, k.in_proj[RANK:, :]).astype(BF16)
+            k.pay[:, RANK:PAY] = (dot_t(conv, last) + tail).astype(BF16)
+        for d, (o, place) in enumerate(zip(others_x, place_x)):
+            src = k.pay.at[pl.ds(pl.multiple_of(o * 64, 64), 64), CUTS[h] : CUTS[h + 1]]
+            copy = remote(src, rx[h].at[x], k.x_s.at[h, d], k.x_r.at[h, x], place)
+            copy.start()
+            x_copies.append(copy)
 
     factor = HD**-0.5 * LOG2E
 
@@ -329,19 +326,20 @@
     causal = iota((ROWS, ROWS), 1) <= iota((ROWS, ROWS), 0)
     attend(k.pair[:, 0:HD], k.pair[:, HD:], causal & (seg_row == k.ext_seg[8:, 0:1]), True)
 
-    z_copies = [
-        remote(k.chunk.at[o], k.rz.at[z], k.z_s.at[o], k.z_r.at[z], {"tp": x * NZ + o}) for o in range(NZ)
-    ]
+    z_copies = []
     for h in range(2):
         for o in others_x:
-            remote(k.rx.at[h, o], k.rx.at[h, o], k.x_s.at[h, 0], k.x_r.at[h, o], place_x[0]).wait_recv()
-        summed = k.pay[pl.ds(pl.multiple_of(x * 64, 64), 64), HALF * h : HALF * (h + 1)].astype(F32)
+            remote(rx[h].at[o], rx[h].at[o], k.x_s.at[h, 0], k.x_r.at[h, o], place_x[0]).wait_recv()
+        summed = k.pay[pl.ds(pl.multiple_of(x * 64, 64), 64), CUTS[h] : CUTS[h + 1]].astype(F32)
         for o in others_x:
-            summed = summed + k.rx[h, o].astype(F32)
+            summed = summed + rx[h][o].astype(F32)
         for r in range(4):
-            k.chunk[4 * h + r] = summed[16 * r : 16 * r + 16, :].astype(BF16)
+            chunk[h][r] = summed[16 * r : 16 * r + 16, :].astype(BF16)
         for r in range(4):
-            pl.when(z != 4 * h + r)(z_copies[4 * h + r].start)
+            o = 4 * h + r
+            copy = remote(chunk[h].at[r], rz[h].at[z], k.z_s.at[o], k.z_r.at[z], {"tp": x * NZ + o})
+            z_copies.append((z != o, copy))
+            pl.when(z != o)(copy.start)
 
     loads["z"].wait()
     gate = k.in_z[...].astype(F32)
@@ -353,29 +351,45 @@
         remote(k.pair, k.kv_all.at[grp - 1], k.kv_s.at[0], k.kv_r.at[grp - 1], twin).wait_recv()
         attend_block(grp - 1)
 
-    for o in others_z:
-        remote(k.chunk.at[0], k.rz.at[o], k.z_s.at[0], k.z_r.at[o], place_z[0]).wait_recv()
-    summed = k.chunk[z].astype(F32)
-    for o in others_z:
-        summed = summed + k.rz[o].astype(F32)
-    k.low[x, z] = summed.astype(BF16)
-    g_copies = []
-    for d, place in enumerate(place_z):
-        g_copies.append(remote(k.low.at[x, z], k.low.at[x, z], k.g_s.at[d], k.g_r.at[z], place))
-    for copy in g_copies:
-        copy.start()
-    h_copies = []
-
-    def forward(o):
-        for d, place in enumerate(place_x):
-            copy = remote(k.low.at[x, o], k.low.at[x, o], k.h_s.at[o, d], k.h_r.at[x, o], place)
-            copy.start()
-            h_copies.append(copy)
-
-    forward(z)
-    for o in others_z:
-        remote(k.low.at[x, z], k.low.at[x, o], k.g_s.at[0], k.g_r.at[o], place_z[0]).wait_recv()
-        forward(o)
+    quarter = lax.rem(z, 4)
+
+    def gathering(h, r, source):
+        piece = low[h].at[x, r]
+        return [remote(piece, piece, k.g_s.at[d], k.g_r.at[source], place) for d, place in enumerate(place_z)]
+
+    def forwards(h, r, source):
+        piece = low[h].at[x, r]
+        return [
+            remote(piece, piece, k.h_s.at[source, d], k.h_r.at[x, source], place)
+            for d, place in enumerate(place_x)
+        ]
+
+    for h in range(2):
+
+        @pl.when(z // 4 == h)
+        def _(h=h):
+            for o in others_z:
+                remote(chunk[h].at[0], rz[h].at[o], k.z_s.at[0], k.z_r.at[o], place_z[0]).wait_recv()
+            summed = chunk[h][quarter].astype(F32)
+            for o in others_z:
+                summed = summed + rz[h][o].astype(F32)
+            low[h][x, quarter] = summed.astype(BF16)
+            for copy in gathering(h, quarter, z) + forwards(h, quarter, z):
+                copy.start()
+
+    for near in range(2):
+
+        @pl.when(z // 4 == near)
+        def _(near=near):
+            for h in (near, 1 - near):
+                for r in range(4):
+
+                    @pl.when(z != 4 * h + r)
+                    def _(h=h, r=r):
+                        piece = low[h].at[x, r]
+                        remote(piece, piece, k.g_s.at[0], k.g_r.at[4 * h + r], place_z[0]).wait_recv()
+                        for copy in forwards(h, r, 4 * h + r):
+                            copy.start()
 
     lax.fori_loop(0, 2 * chip, swap_start, 0)
 
@@ -394,14 +408,15 @@
         loads[n].wait()
     for o in others_x:
         for p in range(NZ):
-            remote(k.low.at[x, p], k.low.at[o, p], k.h_s.at[0, 0], k.h_r.at[o, p], place_x[0]).wait_recv()
+            piece = low[p // 4].at[o, p % 4]
+            remote(piece, piece, k.h_s.at[0, 0], k.h_r.at[o, p], place_x[0]).wait_recv()
     gain = k.in_gain[...].reshape(1, RANK + 2 * NST)
-    left = k.low[:, 0:4].reshape(ROWS, HALF).astype(F32)
-    right = k.low[:, 4:8].reshape(ROWS, HALF).astype(F32)
+    left = k.low0[...].reshape(ROWS, WIDE[0]).astype(F32)
+    right = k.low1[...].reshape(ROWS, WIDE[1]).astype(F32)
     mean = jnp.sum(left * left, axis=1, keepdims=True) + jnp.sum(right[:, :128] * right[:, :128], axis=1, keepdims=True)
     scale = lax.rsqrt(mean / RANK + EPS)
-    k.rank[:, 0:HALF] = (left * scale * gain[:, 0:HALF]).astype(BF16)
-    k.rank[:, HALF:RANK] = (right[:, :128] * scale * gain[:, HALF:RANK]).astype(BF16)
+    k.rank[:, 0:384] = (left * scale * gain[:, 0:384]).astype(BF16)
+    k.rank[:, 384:RANK] = (right[:, :128] * scale * gain[:, 384:RANK]).astype(BF16)
     both = right[:, 128 : 128 + 2 * NST]
     is_b = iota((ROWS, 2 * NST), 1) < NST
     power = both * both
@@ -460,11 +475,11 @@
     for h in range(2):
         k.out_attn[:, h * HD : (h + 1) * HD] = (k.accum[h, :, 0:HD] / k.accum[h, :, HD:]).astype(BF16)
     stores["attn"].start()
-    sums = right[:, 256:384]
-    inverse = lax.rsqrt(sums[:, 16:17] / FEATURES + EPS)
+    sums = right[:, 128:256]
+    inverse = lax.rsqrt(sums[:, SQUARES : SQUARES + 1] / FEATURES + EPS)
     k.out_expert[...] = (k.in_moe[...].astype(F32) * k.in_moe_gain[...] * inverse).astype(BF16)
     logits = (sums * inverse).T
-    experts = iota((LANES, ROWS), 0)
+    experts = iota((LANES, ROWS), 0) - 2 * NST
     first = jnp.sum(jnp.where(experts == k.in_routing[0:1, :], logits, 0.0), axis=0, keepdims=True)
     second = jnp.sum(jnp.where(experts == k.in_routing[1:2, :], logits, 0.0), axis=0, keepdims=True)
     top = jnp.maximum(first, second)
@@ -514,10 +529,20 @@
     for o in others_q:
         theirs = k.out_pages.at[:, 3 - lax.rem(o, 4)]
         remote(theirs, theirs, k.pf_s.at[0], k.pf_r.at[3 - lax.rem(o, 4)], place_q[0]).wait_recv()
-    for copy in list(x_copies.values()) + g_copies + h_copies + page_copies + f_copies + e_copies:
+    for copy in x_copies + page_copies + f_copies + e_copies:
         copy.wait_send()
-    for o in range(NZ):
-        pl.when(z != o)(z_copies[o].wait_send)
+    for here, copy in z_copies:
+        pl.when(here)(copy.wait_send)
+    for h in range(2):
+
+        @pl.when(z // 4 == h)
+        def _(h=h):
+            for copy in gathering(h, quarter, z):
+                copy.wait_send()
+
+    for p in range(NZ):
+        for copy in forwards(p // 4, p % 4, p):
+            copy.wait_send()
     lax.fori_loop(0, 2 * chip, swap_end, 0)
     for here, copy in kv_copies:
         pl.when(here)(copy.wait_send)

time: 60.8 us -> 60 us (0.987)
  Pallas kernels: 60 us -> 59.2 us
    pallas_call x1, Pallas kernels: 58 us -> 57.3 us  [local(): pl.pallas_call(main_kernel, out_shape=shapes, in_specs=[ANY] * len(OPERAN...]
where the time goes in v2:
time: 60 us; the launch traced here: 59.9 us
  Pallas kernels  59.2 us (99%)
  between operations  0.65 us (1%)
    pallas_call x1, Pallas kernels, local(): pl.pallas_call(main_kernel, out_shape=shapes, in_specs=[ANY] * len(OPERAN...  57.3 us
    pallas_call x1, Pallas kernels, local(): pl.pallas_call(hand_out, out_shape=shapes, in_specs=[ANY] * len(OUTPUTS),...  1.95 us

profile of v2, /device:TPU:1, one launch (start us, length us, event | category | flops | bytes accessed | tf_op | source)
XLA Modules:
  0.0 59.9 jit_solution(15756169094829303106)
XLA Ops:
  0.6 57.3 %span.1 = (bf16[256,512]{1,0:T(8,128)(2,1)}, f32[2,512]{1,0:T(2,128)}, bf16[256,256]{1,0:T(8,128)(2,1)}, bf16[8,4,16,256]{3,2,1,0:T(8,128)(2,1)}, bf16[256,256]{1,0:T(8,128)(2,1)}, /*index=5*/f32[2,256]{1,0:T(2,128)}) custom-call(bf16[256,512]{1,0:T(8,128)(2,1)} %refs_0_.1, s32[1,256]{1,0:T(1,128)} %refs_1_.1, f32[4,512]{1,0:T(4,128)} %refs_2_.1, ...), custom_call_target="tpu_custom_call" | custom-call | tf_op jit(solution)/shard_map/span/pallas_call | solution.py:579
  57.9 1.9 %results.1 = (bf16[256,512]{1,0:T(8,128)(2,1)}, f32[2,512]{1,0:T(2,128)}, bf16[256,256]{1,0:T(8,128)(2,1)}, bf16[8,4,16,256]{3,2,1,0:T(8,128)(2,1)}, bf16[256,256]{1,0:T(8,128)(2,1)}, /*index=5*/f32[2,256]{1,0:T(2,128)}) custom-call(bf16[256,512]{1,0:T(8,128)(2,1)} %get-tuple-element.18.refs_0_, f32[2,512]{1,0:T(2,128)} %get-tuple-element.19.refs_1_, ...), custom_call_target="tpu_custom_call" | custom-call | tf_op jit(solution)/shard_map/results/pallas_call | solution.py:593

commit v3 on v2

--- a/solution.py
+++ b/solution.py
@@ -57,7 +57,6 @@
     ("conv_b", (1, WIDTH), F32),
     ("proj", (RANK + 2 * NST, WIDTH), BF16),
     ("owner", (1, 16), I32),
-    ("page", (ROWS, 2, HD), BF16),
     ("pair", (ROWS, 2, HD), BF16),
     ("moe", (ROWS, 256), BF16),
     ("moe_gain", (1, 256), F32),
@@ -79,9 +78,8 @@
     ("expert", (ROWS, 256), BF16),
     ("gate", (2, ROWS), F32),
 )
-OPERANDS = [n for n, _, _ in INPUTS if n not in ("page", "pair")] + ["keys_values"]
+OPERANDS = [n for n, _, _ in INPUTS if n != "pair"] + ["keys_values"]
 SCRATCH = (
-    ("page", (ROWS, 2 * HD), BF16),
     ("pair", (ROWS, 2 * HD), BF16),
     ("rim", (16, WIDTH), BF16),
     ("rim_seg", (8, LANES), F32),
@@ -123,10 +121,10 @@
     ("rim_s", ()), ("rim_r", ()), ("rseg_s", ()), ("rseg_r", ()),
     ("kv_s", (NG,)), ("kv_r", (NG,)), ("sg_s", (NG,)), ("sg_r", (NG,)),
     ("sw_s", (NG,)), ("sw_r", (NG,)),
-    ("pg_s", (NG,)), ("pg_r", (NG,)), ("pf_s", (4,)), ("pf_r", (4,)),
-    ("x_s", (2, NX)), ("x_r", (2, NX)), ("z_s", (NZ,)), ("z_r", (NZ,)),
-    ("g_s", (NZ,)), ("g_r", (NZ,)), ("h_s", (NZ, NX)), ("h_r", (NX, NZ)),
-    ("e_s", (NG,)), ("e_r", (NG,)), ("f_s", ()), ("f_r", ()),
+    ("pg_s", ()), ("pg_r", ()), ("pf_s", ()), ("pf_r", ()),
+    ("x_s", (2,)), ("x_r", (2,)), ("z_s", (2,)), ("z_r", ()),
+    ("g_s", ()), ("g_r", (2,)), ("h_s", (2,)), ("h_r", (2,)),
+    ("e_s", ()), ("e_r", ()), ("f_s", ()), ("f_r", ()),
 )
 
 
@@ -147,11 +145,10 @@
     chip, core = grp // 2, grp % 2
     twin = {"grp": grp + 1 - 2 * core}
     half_rows = pl.ds(pl.multiple_of(128 * core, 128), 128)
-    heads = {"pair": tp // 4, "page": 2 * x + (NZ - 1 - z) // 4}
     loads = {}
     for i, (n, _, _) in enumerate(INPUTS):
-        if n in heads:
-            src = k.hbm_keys_values.at[:, :, pl.ds(pl.multiple_of(heads[n] * HD, HD), HD)]
+        if n == "pair":
+            src = k.hbm_keys_values.at[:, :, pl.ds(pl.multiple_of(tp // 4 * HD, HD), HD)]
         else:
             src = getattr(k, "hbm_" + n)
         loads[n] = pltpu.make_async_copy(src, getattr(k, "in_" + n), k.load.at[i])
@@ -170,9 +167,9 @@
     place_z = [{"tp": x * NZ + o} for o in others_z]
     place_q = [{"tp": x * NZ + o} for o in others_q]
     place_g = [{"grp": o} for o in others_g]
-    place_p = [{"sect": 1 - sect, "tp": x * NZ + (NZ - 1 - z), "grp": o} for o in range(NG)]
+    place_p = [{"sect": 1 - sect, "grp": o} for o in range(NG)]
     across = {"sect": 1 - sect}
-    partners = place_x + place_z + place_g + place_p + [across]
+    partners = place_x + place_z + place_g + place_p
     barrier = pltpu.get_barrier_semaphore()
     for place in partners:
         pl.semaphore_signal(barrier, inc=1, device_id=place, device_id_type=MESH)
@@ -210,7 +207,6 @@
         pl.when(here)(copy.start)
 
     loads["owner"].wait()
-    loads["page"].wait()
     owners = jnp.broadcast_to(k.in_owner[...].astype(F32), (8, 16)).astype(BF16)
     owner_of = dot(owners, (iota((16, ROWS), 0) == iota((16, ROWS), 1) // BLK).astype(BF16))[0:1, :]
     owner_lanes = dot(owners, (iota((16, LANES), 0) == iota((16, LANES), 1)).astype(BF16))[0:1, :]
@@ -220,14 +216,13 @@
     slot = jnp.where(order == lax.rem(z, 4).astype(F32), owner_of, -1.0)
     row, col = iota((NG * BLK, ROWS), 0), iota((NG * BLK, ROWS), 1)
     choose = (slot == (row // BLK).astype(F32)) & (row % BLK == col % BLK)
-    k.page[...] = k.in_page[...].reshape(ROWS, 2 * HD)
-    chosen = dot(jnp.where(choose, 1.0, 0.0).astype(BF16), k.page[...])
+    chosen = dot(jnp.where(choose, 1.0, 0.0).astype(BF16), k.pair[...])
     k.outgoing[...] = chosen.astype(BF16).reshape(NG, BLK, 2 * HD)
-    my_slot, their_slot = lax.rem(z, 4), 3 - lax.rem(z, 4)
+    my_slot = lax.rem(z, 4)
     page_copies = []
     for o in range(NG):
         dst = k.out_pages.at[grp, my_slot]
-        page_copies.append(remote(k.outgoing.at[o], dst, k.pg_s.at[o], k.pg_r.at[grp], place_p[o]))
+        page_copies.append(remote(k.outgoing.at[o], dst, k.pg_s, k.pg_r, place_p[o]))
     for copy in page_copies:
         copy.start()
 
@@ -261,7 +256,6 @@
     conv = k.conv[...]
 
     rx, chunk, rz, low = (k.rx0, k.rx1), (k.chunk0, k.chunk1), (k.rz0, k.rz1), (k.low0, k.low1)
-    x_copies = []
     for h in range(2):
         if h == 0:
             k.pay[:, 0:384] = dot_t(conv, k.in_proj[0:384, :]).astype(BF16)
@@ -270,11 +264,9 @@
             spread = (iota((LANES, 2 * NST), 0) == iota((LANES, 2 * NST), 1)).astype(BF16)
             last = dot(spread, k.in_proj[RANK:, :]).astype(BF16)
             k.pay[:, RANK:PAY] = (dot_t(conv, last) + tail).astype(BF16)
-        for d, (o, place) in enumerate(zip(others_x, place_x)):
+        for o, place in zip(others_x, place_x):
             src = k.pay.at[pl.ds(pl.multiple_of(o * 64, 64), 64), CUTS[h] : CUTS[h + 1]]
-            copy = remote(src, rx[h].at[x], k.x_s.at[h, d], k.x_r.at[h, x], place)
-            copy.start()
-            x_copies.append(copy)
+            remote(src, rx[h].at[x], k.x_s.at[h], k.x_r.at[h], place).start()
 
     factor = HD**-0.5 * LOG2E
 
@@ -326,10 +318,8 @@
     causal = iota((ROWS, ROWS), 1) <= iota((ROWS, ROWS), 0)
     attend(k.pair[:, 0:HD], k.pair[:, HD:], causal & (seg_row == k.ext_seg[8:, 0:1]), True)
 
-    z_copies = []
     for h in range(2):
-        for o in others_x:
-            remote(rx[h].at[o], rx[h].at[o], k.x_s.at[h, 0], k.x_r.at[h, o], place_x[0]).wait_recv()
+        remote(rx[h].at[0:3], rx[h].at[0:3], k.x_s.at[h], k.x_r.at[h], place_x[0]).wait_recv()
         summed = k.pay[pl.ds(pl.multiple_of(x * 64, 64), 64), CUTS[h] : CUTS[h + 1]].astype(F32)
         for o in others_x:
             summed = summed + rx[h][o].astype(F32)
@@ -337,8 +327,7 @@
             chunk[h][r] = summed[16 * r : 16 * r + 16, :].astype(BF16)
         for r in range(4):
             o = 4 * h + r
-            copy = remote(chunk[h].at[r], rz[h].at[z], k.z_s.at[o], k.z_r.at[z], {"tp": x * NZ + o})
-            z_copies.append((z != o, copy))
+            copy = remote(chunk[h].at[r], rz[h].at[z], k.z_s.at[h], k.z_r, {"tp": x * NZ + o})
             pl.when(z != o)(copy.start)
 
     loads["z"].wait()
@@ -352,53 +341,32 @@
         attend_block(grp - 1)
 
     quarter = lax.rem(z, 4)
-
-    def gathering(h, r, source):
-        piece = low[h].at[x, r]
-        return [remote(piece, piece, k.g_s.at[d], k.g_r.at[source], place) for d, place in enumerate(place_z)]
-
-    def forwards(h, r, source):
-        piece = low[h].at[x, r]
-        return [
-            remote(piece, piece, k.h_s.at[source, d], k.h_r.at[x, source], place)
-            for d, place in enumerate(place_x)
-        ]
-
     for h in range(2):
 
         @pl.when(z // 4 == h)
         def _(h=h):
-            for o in others_z:
-                remote(chunk[h].at[0], rz[h].at[o], k.z_s.at[0], k.z_r.at[o], place_z[0]).wait_recv()
+            remote(rz[h].at[0:7], rz[h].at[0:7], k.g_s, k.z_r, place_z[0]).wait_recv()
             summed = chunk[h][quarter].astype(F32)
             for o in others_z:
                 summed = summed + rz[h][o].astype(F32)
             low[h][x, quarter] = summed.astype(BF16)
-            for copy in gathering(h, quarter, z) + forwards(h, quarter, z):
-                copy.start()
-
-    for near in range(2):
-
-        @pl.when(z // 4 == near)
-        def _(near=near):
-            for h in (near, 1 - near):
-                for r in range(4):
-
-                    @pl.when(z != 4 * h + r)
-                    def _(h=h, r=r):
-                        piece = low[h].at[x, r]
-                        remote(piece, piece, k.g_s.at[0], k.g_r.at[4 * h + r], place_z[0]).wait_recv()
-                        for copy in forwards(h, r, 4 * h + r):
-                            copy.start()
+            piece = low[h].at[x, quarter]
+            for place in place_z:
+                remote(piece, piece, k.g_s, k.g_r.at[h], place).start()
+            for part in (h, 1 - h):
+                whole = low[part].at[x]
+                landing = low[part].at[x, 0:3] if part == h else whole
+                remote(landing, landing, k.g_s, k.g_r.at[part], place_z[0]).wait_recv()
+                for place in place_x:
+                    remote(whole, whole, k.h_s.at[part], k.h_r.at[part], place).start()
 
     lax.fori_loop(0, 2 * chip, swap_start, 0)
 
-    for o in range(NG):
-        remote(k.outgoing.at[0], k.out_pages.at[o, their_slot], k.pg_s.at[0], k.pg_r.at[o], place_p[0]).wait_recv()
+    remote(k.outgoing, k.outgoing, k.pg_s, k.pg_r, place_p[0]).wait_recv()
     f_copies = []
     for d, place in enumerate(place_q):
-        mine = k.out_pages.at[:, their_slot]
-        f_copies.append(remote(mine, mine, k.pf_s.at[d], k.pf_r.at[their_slot], place))
+        mine = k.out_pages.at[:, my_slot]
+        f_copies.append(remote(mine, mine, k.pf_s, k.pf_r, place))
     for copy in f_copies:
         copy.start()
 
@@ -406,10 +374,8 @@
 
     for n in ("gain", "dt", "dt_bias", "a_log", "skip", "routing"):
         loads[n].wait()
-    for o in others_x:
-        for p in range(NZ):
-            piece = low[p // 4].at[o, p % 4]
-            remote(piece, piece, k.h_s.at[0, 0], k.h_r.at[o, p], place_x[0]).wait_recv()
+    for h in range(2):
+        remote(low[h].at[0:3], low[h].at[0:3], k.h_s.at[h], k.h_r.at[h], place_x[0]).wait_recv()
     gain = k.in_gain[...].reshape(1, RANK + 2 * NST)
     left = k.low0[...].reshape(ROWS, WIDE[0]).astype(F32)
     right = k.low1[...].reshape(ROWS, WIDE[1]).astype(F32)
@@ -464,11 +430,8 @@
         parts += [part[:, i * LANES : (i + 1) * LANES] for i in range(4)]
         steps = steps - part
     k.own_end[64:80, :] = jnp.concatenate(parts + [jnp.zeros((4, LANES), F32)], axis=0).astype(BF16)
-    e_copies = []
-    for d, place in enumerate(place_g):
-        e_copies.append(remote(k.own_end, k.ends.at[grp], k.e_s.at[d], k.e_r.at[grp], place))
-    for copy in e_copies:
-        copy.start()
+    for place in place_g:
+        remote(k.own_end, k.ends.at[grp], k.e_s, k.e_r, place).start()
     k.ends[grp] = k.own_end[...]
 
     lax.fori_loop(jnp.minimum(2 * chip, 3), 2 * chip, earlier, 0)
@@ -489,8 +452,7 @@
     stores["expert"].start()
     stores["gate"].start()
 
-    for o in others_g:
-        remote(k.own_end, k.ends.at[o], k.e_s.at[0], k.e_r.at[o], place_g[0]).wait_recv()
+    remote(k.ends.at[0:7], k.ends.at[0:7], k.e_s, k.e_r, place_g[0]).wait_recv()
     sums_of = []
     for j in range(NG):
         part = k.ends[j, 64:80, :].astype(F32)
@@ -526,23 +488,23 @@
     for i in range(4):
         k.out_final[:, i * LANES : (i + 1) * LANES] = k.landed[2 * i : 2 * i + 2, :]
     stores["final"].start()
-    for o in others_q:
-        theirs = k.out_pages.at[:, 3 - lax.rem(o, 4)]
-        remote(theirs, theirs, k.pf_s.at[0], k.pf_r.at[3 - lax.rem(o, 4)], place_q[0]).wait_recv()
-    for copy in x_copies + page_copies + f_copies + e_copies:
-        copy.wait_send()
-    for here, copy in z_copies:
-        pl.when(here)(copy.wait_send)
+    rest = k.out_pages.at[:, 0:3]
+    remote(rest, rest, k.pf_s, k.pf_r, place_q[0]).wait()
+    remote(k.outgoing, k.outgoing, k.pg_s, k.pg_r, place_p[0]).wait_send()
+    remote(k.ends.at[0:7], k.ends.at[0:7], k.e_s, k.e_r, place_g[0]).wait_send()
     for h in range(2):
+        remote(rx[h].at[0:3], rx[h].at[0:3], k.x_s.at[h], k.x_r.at[h], place_x[0]).wait_send()
+        remote(low[h].at[0:3], low[h].at[0:3], k.h_s.at[h], k.h_r.at[h], place_x[0]).wait_send()
 
         @pl.when(z // 4 == h)
         def _(h=h):
-            for copy in gathering(h, quarter, z):
-                copy.wait_send()
-
-    for p in range(NZ):
-        for copy in forwards(p // 4, p % 4, p):
-            copy.wait_send()
+            remote(rz[h].at[0:7], rz[h].at[0:7], k.g_s, k.g_r.at[h], place_z[0]).wait_send()
+            remote(rz[h].at[0:3], rz[h].at[0:3], k.z_s.at[h], k.z_r, place_z[0]).wait_send()
+
+        @pl.when(z // 4 != h)
+        def _(h=h):
+            remote(rz[h].at[0:4], rz[h].at[0:4], k.z_s.at[h], k.z_r, place_z[0]).wait_send()
+
     lax.fori_loop(0, 2 * chip, swap_end, 0)
     for here, copy in kv_copies:
         pl.when(here)(copy.wait_send)

time: 60 us -> 60.3 us (level)
  no operation moved by 1% of the time
where the time goes in v3:
time: 60.3 us; the launch traced here: 60.1 us
  Pallas kernels  59.5 us (99%)
  between operations  0.65 us (1%)
    pallas_call x1, Pallas kernels, local(): pl.pallas_call(main_kernel, out_shape=shapes, in_specs=[ANY] * len(OPERAN...  57.5 us
    pallas_call x1, Pallas kernels, local(): pl.pallas_call(hand_out, out_shape=shapes, in_specs=[ANY] * len(OUTPUTS),...  1.95 us

profile of v3, /device:TPU:1, one launch (start us, length us, event | category | flops | bytes accessed | tf_op | source)
XLA Modules:
  0.0 60.1 jit_solution(12324942679288466995)
XLA Ops:
  0.6 57.5 %span.1 = (bf16[256,512]{1,0:T(8,128)(2,1)}, f32[2,512]{1,0:T(2,128)}, bf16[256,256]{1,0:T(8,128)(2,1)}, bf16[8,4,16,256]{3,2,1,0:T(8,128)(2,1)}, bf16[256,256]{1,0:T(8,128)(2,1)}, /*index=5*/f32[2,256]{1,0:T(2,128)}) custom-call(bf16[256,512]{1,0:T(8,128)(2,1)} %refs_0_.1, s32[1,256]{1,0:T(1,128)} %refs_1_.1, f32[4,512]{1,0:T(4,128)} %refs_2_.1, ...), custom_call_target="tpu_custom_call" | custom-call | tf_op jit(solution)/shard_map/span/pallas_call | solution.py:541
  58.2 1.9 %results.1 = (bf16[256,512]{1,0:T(8,128)(2,1)}, f32[2,512]{1,0:T(2,128)}, bf16[256,256]{1,0:T(8,128)(2,1)}, bf16[8,4,16,256]{3,2,1,0:T(8,128)(2,1)}, bf16[256,256]{1,0:T(8,128)(2,1)}, /*index=5*/f32[2,256]{1,0:T(2,128)}) custom-call(bf16[256,512]{1,0:T(8,128)(2,1)} %get-tuple-element.18.refs_0_, f32[2,512]{1,0:T(2,128)} %get-tuple-element.19.refs_1_, ...), custom_call_target="tpu_custom_call" | custom-call | tf_op jit(solution)/shard_map/results/pallas_call | solution.py:555

commit v4 on v3

--- a/solution.py
+++ b/solution.py
@@ -25,6 +25,7 @@
 FEATURES = 8192
 EPS = 1e-06
 SQUARES = 2 * NST + 16
+FIRST = 2
 LOG2E = 1.4426950408889634
 HUGE = 1e30
 VMEM = pl.BlockSpec(memory_space=pltpu.VMEM)
@@ -97,8 +98,7 @@
     ("chunk1", (4, 16, WIDE[1]), BF16),
     ("rz0", (NZ, 16, WIDE[0]), BF16),
     ("rz1", (NZ, 16, WIDE[1]), BF16),
-    ("low0", (NX, 4, 16, WIDE[0]), BF16),
-    ("low1", (NX, 4, 16, WIDE[1]), BF16),
+    ("low", (NX, 4, 16, PAY), BF16),
     ("outgoing", (NG, BLK, 2 * HD), BF16),
     ("best", (2, ROWS, LANES), F32),
     ("accum", (2, ROWS, 2 * HD), F32),
@@ -122,8 +122,8 @@
     ("kv_s", (NG,)), ("kv_r", (NG,)), ("sg_s", (NG,)), ("sg_r", (NG,)),
     ("sw_s", (NG,)), ("sw_r", (NG,)),
     ("pg_s", ()), ("pg_r", ()), ("pf_s", ()), ("pf_r", ()),
-    ("x_s", (2,)), ("x_r", (2,)), ("z_s", (2,)), ("z_r", ()),
-    ("g_s", ()), ("g_r", (2,)), ("h_s", (2,)), ("h_r", (2,)),
+    ("x_s", (2,)), ("x_r", (2,)), ("z_s", (2,)), ("z_r", (2,)),
+    ("g_s", (NZ,)), ("g_r", (4,)), ("h_s", ()), ("h_r", ()),
     ("e_s", ()), ("e_r", ()), ("f_s", ()), ("f_r", ()),
 )
 
@@ -255,7 +255,7 @@
         k.conv[:, cols] = (value / (1.0 + jnp.exp(-value))).astype(BF16)
     conv = k.conv[...]
 
-    rx, chunk, rz, low = (k.rx0, k.rx1), (k.chunk0, k.chunk1), (k.rz0, k.rz1), (k.low0, k.low1)
+    rx, chunk, rz, low = (k.rx0, k.rx1), (k.chunk0, k.chunk1), (k.rz0, k.rz1), k.low
     for h in range(2):
         if h == 0:
             k.pay[:, 0:384] = dot_t(conv, k.in_proj[0:384, :]).astype(BF16)
@@ -270,10 +270,8 @@
 
     factor = HD**-0.5 * LOG2E
 
-    ones = jnp.ones((ROWS, HD), BF16)
-
     def attend(key_block, value_block, allowed, first):
-        valued = jnp.concatenate([value_block, ones], axis=1)
+        valued = jnp.concatenate([value_block, jnp.ones_like(value_block)], axis=1)
         for h in range(2):
             scores = dot_t(k.in_q[:, h * HD : (h + 1) * HD], key_block)
             masked = jnp.where(allowed, scores, -HUGE)
@@ -290,10 +288,9 @@
                 k.accum[h] = k.accum[h] * fade + dot(weights.astype(BF16), valued)
             k.best[h] = jnp.broadcast_to(new, (ROWS, LANES))
 
-    def attend_block(j):
+    def ids_of(j):
         remote(k.seg_out, k.seg_all.at[j], k.sg_s.at[0], k.sg_r.at[j], place_g[0]).wait_recv()
-        same = k.seg_all[j, 0:1, :] == k.ext_seg[8:, 0:1]
-        attend(k.kv_all[j, :, 0:HD], k.kv_all[j, :, HD:], same, False)
+        return k.seg_all[j, 0:1, :]
 
     def swap(i):
         block = k.kv_all.at[2 * chip - 1 - i, half_rows]
@@ -310,8 +307,12 @@
         return carry
 
     def earlier(i, carry):
-        swap(i).wait_recv()
-        attend_block(2 * chip - 1 - i)
+        pair = 2 * (chip - 1 - i)
+        swap(2 * i).wait_recv()
+        swap(2 * i + 1).wait_recv()
+        same = jnp.concatenate([ids_of(pair), ids_of(pair + 1)], axis=1) == k.ext_seg[8:, 0:1]
+        block = k.kv_all[pl.ds(pair, 2)].reshape(2 * ROWS, 2 * HD)
+        attend(block[:, 0:HD], block[:, HD:], same, False)
         return carry
 
     loads["q"].wait()
@@ -326,9 +327,8 @@
         for r in range(4):
             chunk[h][r] = summed[16 * r : 16 * r + 16, :].astype(BF16)
         for r in range(4):
-            o = 4 * h + r
-            copy = remote(chunk[h].at[r], rz[h].at[z], k.z_s.at[h], k.z_r, {"tp": x * NZ + o})
-            pl.when(z != o)(copy.start)
+            copy = remote(chunk[h].at[r], rz[h].at[z], k.z_s.at[h], k.z_r.at[h], {"tp": x * NZ + FIRST + r})
+            pl.when(z != FIRST + r)(copy.start)
 
     loads["z"].wait()
     gate = k.in_z[...].astype(F32)
@@ -338,27 +338,58 @@
     @pl.when(core == 1)
     def _():
         remote(k.pair, k.kv_all.at[grp - 1], k.kv_s.at[0], k.kv_r.at[grp - 1], twin).wait_recv()
-        attend_block(grp - 1)
-
-    quarter = lax.rem(z, 4)
-    for h in range(2):
-
-        @pl.when(z // 4 == h)
-        def _(h=h):
-            remote(rz[h].at[0:7], rz[h].at[0:7], k.g_s, k.z_r, place_z[0]).wait_recv()
+        same = ids_of(grp - 1) == k.ext_seg[8:, 0:1]
+        attend(k.kv_all[grp - 1, :, 0:HD], k.kv_all[grp - 1, :, HD:], same, False)
+
+    is_owner = (z >= FIRST) & (z < FIRST + 4)
+    quarter = jnp.clip(z - FIRST, 0, 3)
+
+    def forward(r):
+        piece = low.at[x, r]
+        for place in place_x:
+            remote(piece, piece, k.h_s, k.h_r, place).start()
+
+    loads["gain"].wait()
+
+    @pl.when(is_owner)
+    def _():
+        sums = []
+        for h in range(2):
+            remote(rz[h].at[0:7], rz[h].at[0:7], k.z_s.at[h], k.z_r.at[h], place_z[0]).wait_recv()
             summed = chunk[h][quarter].astype(F32)
             for o in others_z:
                 summed = summed + rz[h][o].astype(F32)
-            low[h][x, quarter] = summed.astype(BF16)
-            piece = low[h].at[x, quarter]
-            for place in place_z:
-                remote(piece, piece, k.g_s, k.g_r.at[h], place).start()
-            for part in (h, 1 - h):
-                whole = low[part].at[x]
-                landing = low[part].at[x, 0:3] if part == h else whole
-                remote(landing, landing, k.g_s, k.g_r.at[part], place_z[0]).wait_recv()
-                for place in place_x:
-                    remote(whole, whole, k.h_s.at[part], k.h_r.at[part], place).start()
+            sums.append(summed)
+        left, right = sums
+        rank, last = right[:, 0:128], right[:, 128:256]
+        gain = k.in_gain[...].reshape(1, RANK + 2 * NST)
+        mean = jnp.sum(left * left, axis=1, keepdims=True) + jnp.sum(rank * rank, axis=1, keepdims=True)
+        scale = lax.rsqrt(mean / RANK + EPS)
+        low[x, quarter, :, 0:384] = (left * scale * gain[:, 0:384]).astype(BF16)
+        low[x, quarter, :, 384:RANK] = (rank * scale * gain[:, 384:RANK]).astype(BF16)
+        lanes = iota((16, LANES), 1)
+        power = last * last
+        mean_b = jnp.sum(jnp.where(lanes < NST, power, 0.0), axis=1, keepdims=True) / NST
+        mean_c = jnp.sum(jnp.where((lanes >= NST) & (lanes < 2 * NST), power, 0.0), axis=1, keepdims=True) / NST
+        inverse = lax.rsqrt(last[:, SQUARES : SQUARES + 1] / FEATURES + EPS)
+        coarse = inverse.astype(BF16).astype(F32)
+        scale = jnp.where(lanes < NST, lax.rsqrt(mean_b + EPS), lax.rsqrt(mean_c + EPS))
+        last = last * jnp.where(lanes < 2 * NST, scale, inverse)
+        last = jnp.where(lanes == SQUARES, coarse, jnp.where(lanes == SQUARES + 1, inverse - coarse, last))
+        low[x, quarter, :, RANK:PAY] = last.astype(BF16)
+        low[x, quarter, :, RANK : RANK + 2 * NST] = (last[:, 0 : 2 * NST] * gain[:, RANK:]).astype(BF16)
+        piece = low.at[x, quarter]
+        for d, place in enumerate(place_z):
+            remote(piece, piece, k.g_s.at[d], k.g_r.at[quarter], place).start()
+        forward(quarter)
+
+    for r in range(4):
+
+        @pl.when(z != FIRST + r)
+        def _(r=r):
+            piece = low.at[x, r]
+            remote(piece, piece, k.g_s.at[0], k.g_r.at[r], place_z[0]).wait_recv()
+            forward(r)
 
     lax.fori_loop(0, 2 * chip, swap_start, 0)
 
@@ -370,26 +401,13 @@
     for copy in f_copies:
         copy.start()
 
-    lax.fori_loop(0, jnp.minimum(2 * chip, 3), earlier, 0)
-
-    for n in ("gain", "dt", "dt_bias", "a_log", "skip", "routing"):
+
+    for n in ("dt", "dt_bias", "a_log", "skip", "routing"):
         loads[n].wait()
-    for h in range(2):
-        remote(low[h].at[0:3], low[h].at[0:3], k.h_s.at[h], k.h_r.at[h], place_x[0]).wait_recv()
-    gain = k.in_gain[...].reshape(1, RANK + 2 * NST)
-    left = k.low0[...].reshape(ROWS, WIDE[0]).astype(F32)
-    right = k.low1[...].reshape(ROWS, WIDE[1]).astype(F32)
-    mean = jnp.sum(left * left, axis=1, keepdims=True) + jnp.sum(right[:, :128] * right[:, :128], axis=1, keepdims=True)
-    scale = lax.rsqrt(mean / RANK + EPS)
-    k.rank[:, 0:384] = (left * scale * gain[:, 0:384]).astype(BF16)
-    k.rank[:, 384:RANK] = (right[:, :128] * scale * gain[:, 384:RANK]).astype(BF16)
-    both = right[:, 128 : 128 + 2 * NST]
-    is_b = iota((ROWS, 2 * NST), 1) < NST
-    power = both * both
-    mean_b = jnp.sum(jnp.where(is_b, power, 0.0), axis=1, keepdims=True) / NST
-    mean_c = jnp.sum(jnp.where(is_b, 0.0, power), axis=1, keepdims=True) / NST
-    scale = jnp.where(is_b, lax.rsqrt(mean_b + EPS), lax.rsqrt(mean_c + EPS))
-    k.bc[...] = (both * scale * gain[:, RANK : RANK + 2 * NST]).astype(BF16)
+    remote(low.at[0:3], low.at[0:3], k.h_s, k.h_r, place_x[0]).wait_recv()
+    k.rank[...] = low[...].reshape(ROWS, PAY)[:, 0:RANK]
+    shared = low[...].reshape(ROWS, PAY)[:, RANK:PAY]
+    k.bc[...] = shared[:, 0 : 2 * NST]
 
     raw = dot(k.rank[...], k.in_dt[...]) + k.in_dt_bias[...]
     step = jnp.maximum(raw, 0.0) + jnp.log(1.0 + jnp.exp(-jnp.abs(raw)))
@@ -434,14 +452,14 @@
         remote(k.own_end, k.ends.at[grp], k.e_s, k.e_r, place).start()
     k.ends[grp] = k.own_end[...]
 
-    lax.fori_loop(jnp.minimum(2 * chip, 3), 2 * chip, earlier, 0)
+    lax.fori_loop(0, chip, earlier, 0)
     for h in range(2):
         k.out_attn[:, h * HD : (h + 1) * HD] = (k.accum[h, :, 0:HD] / k.accum[h, :, HD:]).astype(BF16)
     stores["attn"].start()
-    sums = right[:, 128:256]
-    inverse = lax.rsqrt(sums[:, SQUARES : SQUARES + 1] / FEATURES + EPS)
+    shared = shared.astype(F32)
+    inverse = shared[:, SQUARES : SQUARES + 1] + shared[:, SQUARES + 1 : SQUARES + 2]
     k.out_expert[...] = (k.in_moe[...].astype(F32) * k.in_moe_gain[...] * inverse).astype(BF16)
-    logits = (sums * inverse).T
+    logits = shared.T
     experts = iota((LANES, ROWS), 0) - 2 * NST
     first = jnp.sum(jnp.where(experts == k.in_routing[0:1, :], logits, 0.0), axis=0, keepdims=True)
     second = jnp.sum(jnp.where(experts == k.in_routing[1:2, :], logits, 0.0), axis=0, keepdims=True)
@@ -494,16 +512,21 @@
     remote(k.ends.at[0:7], k.ends.at[0:7], k.e_s, k.e_r, place_g[0]).wait_send()
     for h in range(2):
         remote(rx[h].at[0:3], rx[h].at[0:3], k.x_s.at[h], k.x_r.at[h], place_x[0]).wait_send()
-        remote(low[h].at[0:3], low[h].at[0:3], k.h_s.at[h], k.h_r.at[h], place_x[0]).wait_send()
-
-        @pl.when(z // 4 == h)
+
+        @pl.when(is_owner)
         def _(h=h):
-            remote(rz[h].at[0:7], rz[h].at[0:7], k.g_s, k.g_r.at[h], place_z[0]).wait_send()
-            remote(rz[h].at[0:3], rz[h].at[0:3], k.z_s.at[h], k.z_r, place_z[0]).wait_send()
-
-        @pl.when(z // 4 != h)
+            remote(rz[h].at[0:3], rz[h].at[0:3], k.z_s.at[h], k.z_r.at[h], place_z[0]).wait_send()
+
+        @pl.when(jnp.logical_not(is_owner))
         def _(h=h):
-            remote(rz[h].at[0:4], rz[h].at[0:4], k.z_s.at[h], k.z_r, place_z[0]).wait_send()
+            remote(rz[h].at[0:4], rz[h].at[0:4], k.z_s.at[h], k.z_r.at[h], place_z[0]).wait_send()
+
+    remote(low.at[0:3], low.at[0:3], k.h_s, k.h_r, place_x[0]).wait_send()
+
+    @pl.when(is_owner)
+    def _():
+        for d in range(NZ - 1):
+            remote(low.at[x, 0], low.at[x, 0], k.g_s.at[d], k.g_r.at[0], place_z[0]).wait_send()
 
     lax.fori_loop(0, 2 * chip, swap_end, 0)
     for here, copy in kv_copies:

time: 60.3 us -> 60.2 us (level)
  no operation moved by 1% of the time
where the time goes in v4:
time: 60.2 us; the launch traced here: 60.1 us
  Pallas kernels  59.4 us (99%)
  between operations  0.65 us (1%)
    pallas_call x1, Pallas kernels, local(): pl.pallas_call(main_kernel, out_shape=shapes, in_specs=[ANY] * len(OPERAN...  57.5 us
    pallas_call x1, Pallas kernels, local(): pl.pallas_call(hand_out, out_shape=shapes, in_specs=[ANY] * len(OUTPUTS),...  1.95 us

profile of v4, /device:TPU:1, one launch (start us, length us, event | category | flops | bytes accessed | tf_op | source)
XLA Modules:
  0.0 60.1 jit_solution(14616017785515156700)
XLA Ops:
  0.6 57.5 %span.1 = (bf16[256,512]{1,0:T(8,128)(2,1)}, f32[2,512]{1,0:T(2,128)}, bf16[256,256]{1,0:T(8,128)(2,1)}, bf16[8,4,16,256]{3,2,1,0:T(8,128)(2,1)}, bf16[256,256]{1,0:T(8,128)(2,1)}, /*index=5*/f32[2,256]{1,0:T(2,128)}) custom-call(bf16[256,512]{1,0:T(8,128)(2,1)} %refs_0_.1, s32[1,256]{1,0:T(1,128)} %refs_1_.1, f32[4,512]{1,0:T(4,128)} %refs_2_.1, ...), custom_call_target="tpu_custom_call" | custom-call | tf_op jit(solution)/shard_map/span/pallas_call | solution.py:564
  58.1 1.9 %results.1 = (bf16[256,512]{1,0:T(8,128)(2,1)}, f32[2,512]{1,0:T(2,128)}, bf16[256,256]{1,0:T(8,128)(2,1)}, bf16[8,4,16,256]{3,2,1,0:T(8,128)(2,1)}, bf16[256,256]{1,0:T(8,128)(2,1)}, /*index=5*/f32[2,256]{1,0:T(2,128)}) custom-call(bf16[256,512]{1,0:T(8,128)(2,1)} %get-tuple-element.18.refs_0_, f32[2,512]{1,0:T(2,128)} %get-tuple-element.19.refs_1_, ...), custom_call_target="tpu_custom_call" | custom-call | tf_op jit(solution)/shard_map/results/pallas_call | solution.py:578

commit v5 on v4

--- a/solution.py
+++ b/solution.py
@@ -191,20 +191,6 @@
 
     loads["pair"].wait()
     k.pair[...] = k.in_pair[...].reshape(ROWS, 2 * HD)
-    kv_copies = []
-    for d in range(1, NG):
-        place = {"grp": lax.rem(grp + d, NG)}
-        copy = remote(k.seg_out, k.seg_all.at[grp], k.sg_s.at[d], k.sg_r.at[grp], place)
-        kv_copies.append((grp + d < NG, copy))
-    for d in range(1, NG // 2):
-        for half in range(2):
-            rows = slice(128 * half, 128 * half + 128)
-            place = {"grp": 2 * lax.rem(chip + d, NG // 2) + half}
-            copy = remote(k.pair.at[rows], k.kv_all.at[grp, rows], k.kv_s.at[2 * d + half], k.kv_r.at[grp], place)
-            kv_copies.append((chip + d < NG // 2, copy))
-    kv_copies.append((core == 0, remote(k.pair, k.kv_all.at[grp], k.kv_s.at[0], k.kv_r.at[grp], twin)))
-    for here, copy in kv_copies:
-        pl.when(here)(copy.start)
 
     loads["owner"].wait()
     owners = jnp.broadcast_to(k.in_owner[...].astype(F32), (8, 16)).astype(BF16)
@@ -223,8 +209,6 @@
     for o in range(NG):
         dst = k.out_pages.at[grp, my_slot]
         page_copies.append(remote(k.outgoing.at[o], dst, k.pg_s, k.pg_r, place_p[o]))
-    for copy in page_copies:
-        copy.start()
 
     loads["moe"].wait()
     loads["moe_gain"].wait()
@@ -268,6 +252,9 @@
             src = k.pay.at[pl.ds(pl.multiple_of(o * 64, 64), 64), CUTS[h] : CUTS[h + 1]]
             remote(src, rx[h].at[x], k.x_s.at[h], k.x_r.at[h], place).start()
 
+    for copy in page_copies:
+        copy.start()
+
     factor = HD**-0.5 * LOG2E
 
     def attend(key_block, value_block, allowed, first):
@@ -330,16 +317,25 @@
             copy = remote(chunk[h].at[r], rz[h].at[z], k.z_s.at[h], k.z_r.at[h], {"tp": x * NZ + FIRST + r})
             pl.when(z != FIRST + r)(copy.start)
 
+    kv_copies = []
+    for d in range(1, NG):
+        place = {"grp": lax.rem(grp + d, NG)}
+        copy = remote(k.seg_out, k.seg_all.at[grp], k.sg_s.at[d], k.sg_r.at[grp], place)
+        kv_copies.append((grp + d < NG, copy))
+    for d in range(1, NG // 2):
+        for half in range(2):
+            rows = slice(128 * half, 128 * half + 128)
+            place = {"grp": 2 * lax.rem(chip + d, NG // 2) + half}
+            copy = remote(k.pair.at[rows], k.kv_all.at[grp, rows], k.kv_s.at[2 * d + half], k.kv_r.at[grp], place)
+            kv_copies.append((chip + d < NG // 2, copy))
+    kv_copies.append((core == 0, remote(k.pair, k.kv_all.at[grp], k.kv_s.at[0], k.kv_r.at[grp], twin)))
+    for here, copy in kv_copies:
+        pl.when(here)(copy.start)
+
     loads["z"].wait()
     gate = k.in_z[...].astype(F32)
     k.silu_z[...] = gate / (1.0 + jnp.exp(-gate))
 
-
-    @pl.when(core == 1)
-    def _():
-        remote(k.pair, k.kv_all.at[grp - 1], k.kv_s.at[0], k.kv_r.at[grp - 1], twin).wait_recv()
-        same = ids_of(grp - 1) == k.ext_seg[8:, 0:1]
-        attend(k.kv_all[grp - 1, :, 0:HD], k.kv_all[grp - 1, :, HD:], same, False)
 
     is_owner = (z >= FIRST) & (z < FIRST + 4)
     quarter = jnp.clip(z - FIRST, 0, 3)
@@ -391,8 +387,6 @@
             remote(piece, piece, k.g_s.at[0], k.g_r.at[r], place_z[0]).wait_recv()
             forward(r)
 
-    lax.fori_loop(0, 2 * chip, swap_start, 0)
-
     remote(k.outgoing, k.outgoing, k.pg_s, k.pg_r, place_p[0]).wait_recv()
     f_copies = []
     for d, place in enumerate(place_q):
@@ -452,10 +446,13 @@
         remote(k.own_end, k.ends.at[grp], k.e_s, k.e_r, place).start()
     k.ends[grp] = k.own_end[...]
 
-    lax.fori_loop(0, chip, earlier, 0)
-    for h in range(2):
-        k.out_attn[:, h * HD : (h + 1) * HD] = (k.accum[h, :, 0:HD] / k.accum[h, :, HD:]).astype(BF16)
-    stores["attn"].start()
+    lax.fori_loop(0, 2 * chip, swap_start, 0)
+    @pl.when(core == 1)
+    def _():
+        remote(k.pair, k.kv_all.at[grp - 1], k.kv_s.at[0], k.kv_r.at[grp - 1], twin).wait_recv()
+        same = ids_of(grp - 1) == k.ext_seg[8:, 0:1]
+        attend(k.kv_all[grp - 1, :, 0:HD], k.kv_all[grp - 1, :, HD:], same, False)
+
     shared = shared.astype(F32)
     inverse = shared[:, SQUARES : SQUARES + 1] + shared[:, SQUARES + 1 : SQUARES + 2]
     k.out_expert[...] = (k.in_moe[...].astype(F32) * k.in_moe_gain[...] * inverse).astype(BF16)
@@ -469,6 +466,10 @@
     k.out_gate[1:2, :] = second / (first + second)
     stores["expert"].start()
     stores["gate"].start()
+    lax.fori_loop(0, chip, earlier, 0)
+    for h in range(2):
+        k.out_attn[:, h * HD : (h + 1) * HD] = (k.accum[h, :, 0:HD] / k.accum[h, :, HD:]).astype(BF16)
+    stores["attn"].start()
 
     remote(k.ends.at[0:7], k.ends.at[0:7], k.e_s, k.e_r, place_g[0]).wait_recv()
     sums_of = []

time: 60.2 us -> 60.8 us (level)
  no operation moved by 1% of the time
where the time goes in v5:
time: 60.8 us; the launch traced here: 60.6 us
  Pallas kernels  60 us (99%)
  between operations  0.65 us (1%)
    pallas_call x1, Pallas kernels, local(): pl.pallas_call(main_kernel, out_shape=shapes, in_specs=[ANY] * len(OPERAN...  58 us
    pallas_call x1, Pallas kernels, local(): pl.pallas_call(hand_out, out_shape=shapes, in_specs=[ANY] * len(OUTPUTS),...  1.95 us

profile of v5, /device:TPU:1, one launch (start us, length us, event | category | flops | bytes accessed | tf_op | source)
XLA Modules:
  0.0 60.6 jit_solution(2278032001563796755)
XLA Ops:
  0.6 58.0 %span.1 = (bf16[256,512]{1,0:T(8,128)(2,1)}, f32[2,512]{1,0:T(2,128)}, bf16[256,256]{1,0:T(8,128)(2,1)}, bf16[8,4,16,256]{3,2,1,0:T(8,128)(2,1)}, bf16[256,256]{1,0:T(8,128)(2,1)}, /*index=5*/f32[2,256]{1,0:T(2,128)}) custom-call(bf16[256,512]{1,0:T(8,128)(2,1)} %refs_0_.1, s32[1,256]{1,0:T(1,128)} %refs_1_.1, f32[4,512]{1,0:T(4,128)} %refs_2_.1, ...), custom_call_target="tpu_custom_call" | custom-call | tf_op jit(solution)/shard_map/span/pallas_call | solution.py:565
  58.7 1.9 %results.1 = (bf16[256,512]{1,0:T(8,128)(2,1)}, f32[2,512]{1,0:T(2,128)}, bf16[256,256]{1,0:T(8,128)(2,1)}, bf16[8,4,16,256]{3,2,1,0:T(8,128)(2,1)}, bf16[256,256]{1,0:T(8,128)(2,1)}, /*index=5*/f32[2,256]{1,0:T(2,128)}) custom-call(bf16[256,512]{1,0:T(8,128)(2,1)} %get-tuple-element.18.refs_0_, f32[2,512]{1,0:T(2,128)} %get-tuple-element.19.refs_1_, ...), custom_call_target="tpu_custom_call" | custom-call | tf_op jit(solution)/shard_map/results/pallas_call | solution.py:579

commit v6 on v5

--- a/solution.py
+++ b/solution.py
@@ -189,27 +189,6 @@
     rim_copy.start()
     rseg_copy.start()
 
-    loads["pair"].wait()
-    k.pair[...] = k.in_pair[...].reshape(ROWS, 2 * HD)
-
-    loads["owner"].wait()
-    owners = jnp.broadcast_to(k.in_owner[...].astype(F32), (8, 16)).astype(BF16)
-    owner_of = dot(owners, (iota((16, ROWS), 0) == iota((16, ROWS), 1) // BLK).astype(BF16))[0:1, :]
-    owner_lanes = dot(owners, (iota((16, LANES), 0) == iota((16, LANES), 1)).astype(BF16))[0:1, :]
-    owner_rows = jnp.broadcast_to(owner_lanes, (LANES, LANES)).T[0:16, 0:1]
-    before = (owner_rows == owner_of) & (iota((16, ROWS), 0) < iota((16, ROWS), 1) // BLK)
-    order = jnp.sum(jnp.where(before, 1.0, 0.0), axis=0, keepdims=True)
-    slot = jnp.where(order == lax.rem(z, 4).astype(F32), owner_of, -1.0)
-    row, col = iota((NG * BLK, ROWS), 0), iota((NG * BLK, ROWS), 1)
-    choose = (slot == (row // BLK).astype(F32)) & (row % BLK == col % BLK)
-    chosen = dot(jnp.where(choose, 1.0, 0.0).astype(BF16), k.pair[...])
-    k.outgoing[...] = chosen.astype(BF16).reshape(NG, BLK, 2 * HD)
-    my_slot = lax.rem(z, 4)
-    page_copies = []
-    for o in range(NG):
-        dst = k.out_pages.at[grp, my_slot]
-        page_copies.append(remote(k.outgoing.at[o], dst, k.pg_s, k.pg_r, place_p[o]))
-
     loads["moe"].wait()
     loads["moe_gain"].wait()
     loads["router"].wait()
@@ -252,6 +231,26 @@
             src = k.pay.at[pl.ds(pl.multiple_of(o * 64, 64), 64), CUTS[h] : CUTS[h + 1]]
             remote(src, rx[h].at[x], k.x_s.at[h], k.x_r.at[h], place).start()
 
+    loads["pair"].wait()
+    k.pair[...] = k.in_pair[...].reshape(ROWS, 2 * HD)
+
+    loads["owner"].wait()
+    owners = jnp.broadcast_to(k.in_owner[...].astype(F32), (8, 16)).astype(BF16)
+    owner_of = dot(owners, (iota((16, ROWS), 0) == iota((16, ROWS), 1) // BLK).astype(BF16))[0:1, :]
+    owner_lanes = dot(owners, (iota((16, LANES), 0) == iota((16, LANES), 1)).astype(BF16))[0:1, :]
+    owner_rows = jnp.broadcast_to(owner_lanes, (LANES, LANES)).T[0:16, 0:1]
+    before = (owner_rows == owner_of) & (iota((16, ROWS), 0) < iota((16, ROWS), 1) // BLK)
+    order = jnp.sum(jnp.where(before, 1.0, 0.0), axis=0, keepdims=True)
+    slot = jnp.where(order == lax.rem(z, 4).astype(F32), owner_of, -1.0)
+    row, col = iota((NG * BLK, ROWS), 0), iota((NG * BLK, ROWS), 1)
+    choose = (slot == (row // BLK).astype(F32)) & (row % BLK == col % BLK)
+    chosen = dot(jnp.where(choose, 1.0, 0.0).astype(BF16), k.pair[...])
+    k.outgoing[...] = chosen.astype(BF16).reshape(NG, BLK, 2 * HD)
+    my_slot = lax.rem(z, 4)
+    page_copies = []
+    for o in range(NG):
+        dst = k.out_pages.at[grp, my_slot]
+        page_copies.append(remote(k.outgoing.at[o], dst, k.pg_s, k.pg_r, place_p[o]))
     for copy in page_copies:
         copy.start()
 

time: 60.8 us -> 60.8 us (level)
  no operation moved by 1% of the time
where the time goes in v6:
time: 60.8 us; the launch traced here: 60.6 us
  Pallas kernels  60 us (99%)
  between operations  0.65 us (1%)
    pallas_call x1, Pallas kernels, local(): pl.pallas_call(main_kernel, out_shape=shapes, in_specs=[ANY] * len(OPERAN...  58 us
    pallas_call x1, Pallas kernels, local(): pl.pallas_call(hand_out, out_shape=shapes, in_specs=[ANY] * len(OUTPUTS),...  1.95 us

profile of v6, /device:TPU:1, one launch (start us, length us, event | category | flops | bytes accessed | tf_op | source)
XLA Modules:
  0.0 60.6 jit_solution(7711027808079828578)
XLA Ops:
  0.6 58.0 %span.1 = (bf16[256,512]{1,0:T(8,128)(2,1)}, f32[2,512]{1,0:T(2,128)}, bf16[256,256]{1,0:T(8,128)(2,1)}, bf16[8,4,16,256]{3,2,1,0:T(8,128)(2,1)}, bf16[256,256]{1,0:T(8,128)(2,1)}, /*index=5*/f32[2,256]{1,0:T(2,128)}) custom-call(bf16[256,512]{1,0:T(8,128)(2,1)} %refs_0_.1, s32[1,256]{1,0:T(1,128)} %refs_1_.1, f32[4,512]{1,0:T(4,128)} %refs_2_.1, ...), custom_call_target="tpu_custom_call" | custom-call | tf_op jit(solution)/shard_map/span/pallas_call | solution.py:564
  58.7 1.9 %results.1 = (bf16[256,512]{1,0:T(8,128)(2,1)}, f32[2,512]{1,0:T(2,128)}, bf16[256,256]{1,0:T(8,128)(2,1)}, bf16[8,4,16,256]{3,2,1,0:T(8,128)(2,1)}, bf16[256,256]{1,0:T(8,128)(2,1)}, /*index=5*/f32[2,256]{1,0:T(2,128)}) custom-call(bf16[256,512]{1,0:T(8,128)(2,1)} %get-tuple-element.18.refs_0_, f32[2,512]{1,0:T(2,128)} %get-tuple-element.19.refs_1_, ...), custom_call_target="tpu_custom_call" | custom-call | tf_op jit(solution)/shard_map/results/pallas_call | solution.py:578
